TPU v7x, 512 devices: a whole 4x8x8 slice. The times are simulated.
512 devices in a mesh: pairs: 64 (over y, x, core), seg: 8 (over z).
Axes of the slice: x: 4, y: 8, z: 8, core: 2. Of those that a mesh axis runs over, the one named last changes fastest.
Arguments:
- traces: bfloat16 [8, 256, 72000], P('seg', 'pairs')
- block_sources: int32 [64, 26], P('pairs'), may hold values from 0 to 63, as said below
- send_lists: int32 [64, 64, 1], P('pairs'), may hold values from -1 to 3, as said below
Outputs:
- pws: float32 [1600, 3840], P('pairs', 'seg')
Inputs may be any that keep to these rules, and one draw needn't show every extreme that they name: `block_sources`: row b names the devices storing block b's 26 stations in order, the virtual source first. No index stands more than 1 times in a row, and in every row some index stands exactly 1 times. send_lists[d, b, j] is the local index, among the 4 stations stored on device d, of the station at the (j + 1)-th position of row b of block_sources that names d, and -1 where d stands fewer than j + 1 times in that row. The stations of one block are distinct.
All inputs are finite; a program needn't handle non-finite values.
Results may differ from a plain program's by a relative error of at most 0.04.
Values may be sent and summed in bfloat16 or wider, within the bound.
No kernel may reach another device: no remote copies, remote signals or barrier semaphores. Data moves between devices by JAX's collectives and lax.ppermute only.
A program may use at most 128 MiB of HBM per device.

v0:
```python
import math

import jax
import jax.numpy as jnp
from jax import lax
from jax.sharding import PartitionSpec as P

N1 = 240
N2 = 300
KB = 32
H = 8


def angles(left_index, right_index, period):
    product = left_index[:, None] * right_index[None, :] % period
    return product.astype(jnp.float32) * (2.0 * math.pi / period)


def make_tables():
    bins_inner = jnp.arange(N2, dtype=jnp.int32)
    samples_outer = jnp.arange(N1, dtype=jnp.int32)
    band_blocks = jnp.arange(1, KB + 1, dtype=jnp.int32)
    inner_angle = angles(bins_inner, bins_inner, N2)
    inner_table = jnp.concatenate([jnp.cos(inner_angle), -jnp.sin(inner_angle)], 0).astype(
        jnp.bfloat16
    )
    twist_angle = angles(bins_inner, samples_outer, N2 * N1)
    twist_cos = jnp.cos(twist_angle).astype(jnp.bfloat16)
    twist_sin = jnp.sin(twist_angle).astype(jnp.bfloat16)
    outer_angle = angles(samples_outer, band_blocks, N1)
    outer_cos = jnp.cos(outer_angle)
    outer_sin = jnp.sin(outer_angle)
    outer_table = jnp.concatenate(
        [jnp.concatenate([outer_cos, -outer_sin], 1), jnp.concatenate([outer_sin, outer_cos], 1)], 0
    ).astype(jnp.bfloat16)
    back_table = jnp.concatenate(
        [
            jnp.concatenate([outer_cos.T, outer_sin.T], 1),
            jnp.concatenate([-outer_sin.T, outer_cos.T], 1),
        ],
        0,
    ).astype(jnp.bfloat16)
    lag_rows = jnp.arange(-H, H, dtype=jnp.int32) % N2
    lag_angle = angles(lag_rows, bins_inner, N2)
    lag_table = jnp.concatenate([jnp.cos(lag_angle), jnp.sin(lag_angle)], 0).astype(jnp.bfloat16)
    return (inner_table, twist_cos, twist_sin, outer_table, back_table, lag_table)


def whiten(spectra):
    real_part = spectra[..., :KB]
    imag_part = spectra[..., KB:]
    magnitude = jnp.sqrt(real_part * real_part + imag_part * imag_part)
    level_mean = jnp.mean(magnitude, axis=1, keepdims=True) + 1e-06
    return (spectra / jnp.concatenate([level_mean, level_mean], -1)).astype(jnp.bfloat16)


def spectrum(records, tables):
    inner_table, twist_cos, twist_sin, outer_table, back_table, lag_table = tables
    number = records.shape[0]
    folded = records.reshape(number, N2, N1)
    inner_terms = jnp.einsum("kn,tnm->tkm", inner_table, folded, preferred_element_type=jnp.float32)
    real_part = inner_terms[:, :N2]
    imag_part = inner_terms[:, N2:]
    cosine = twist_cos.astype(jnp.float32)
    sine = twist_sin.astype(jnp.float32)
    turned = jnp.concatenate(
        [real_part * cosine + imag_part * sine, imag_part * cosine - real_part * sine], -1
    ).astype(jnp.bfloat16)
    spectra = jnp.einsum("tkm,mf->tkf", turned, outer_table, preferred_element_type=jnp.float32)
    return whiten(spectra)


def spectra_of(records, tables):
    number = records.shape[0]
    halves = records.reshape(2, number // 2, records.shape[1])
    whitened = lax.map(lambda member_group: spectrum(member_group, tables), halves)
    return whitened.reshape(number, N2, 2 * KB)


def lag_partials(source, receivers, tables):
    inner_table, twist_cos, twist_sin, outer_table, back_table, lag_table = tables
    source = source.astype(jnp.float32)
    receivers = receivers.astype(jnp.float32)
    src_real = source[None, :, :KB]
    src_imag = source[None, :, KB:]
    rec_real = receivers[..., :KB]
    rec_imag = receivers[..., KB:]
    correlation = jnp.concatenate(
        [src_real * rec_real + src_imag * rec_imag, src_imag * rec_real - src_real * rec_imag], -1
    ).astype(jnp.bfloat16)
    section_one = jnp.einsum(
        "pkf,fm->pkm", correlation, back_table, preferred_element_type=jnp.float32
    )
    real_part = section_one[..., :N1]
    imag_part = section_one[..., N1:]
    cosine = twist_cos.astype(jnp.float32)
    sine = twist_sin.astype(jnp.float32)
    turned = jnp.concatenate(
        [real_part * cosine - imag_part * sine, real_part * sine + imag_part * cosine], -1
    ).astype(jnp.bfloat16)
    lag_terms = jnp.einsum("jk,pkm->pjm", lag_table, turned, preferred_element_type=jnp.float32)
    normalize = 1.0 / math.sqrt(KB * N2)
    real_lag = (lag_terms[:, : 2 * H, :N1] - lag_terms[:, 2 * H :, N1:]) * normalize
    imag_lag = (lag_terms[:, 2 * H :, :N1] + lag_terms[:, : 2 * H, N1:]) * normalize
    pairs_here = receivers.shape[0]
    real_lag = real_lag.reshape(pairs_here, 2 * H * N1)
    imag_lag = imag_lag.reshape(pairs_here, 2 * H * N1)
    floor_mag = jnp.maximum(jnp.sqrt(real_lag * real_lag + imag_lag * imag_lag), 0.25)
    return jnp.stack([real_lag, real_lag / floor_mag, imag_lag / floor_mag], 0)


def local(traces, block_sources, send_lists):
    tables = make_tables()
    stations = traces[0]
    sources = block_sources[0]
    wanted = send_lists[0]
    peer_count = wanted.shape[0]
    slot_count = wanted.shape[1]
    block_width = sources.shape[0]
    position = jnp.arange(block_width, dtype=jnp.int32)
    earlier = (sources[:, None] == sources[None, :]) & (position[:, None] > position[None, :])
    repeats = jnp.sum(earlier.astype(jnp.int32), axis=1)
    arrival_rows = sources * slot_count + repeats
    present = (wanted >= 0)[:, :, None]
    chosen = jnp.maximum(wanted, 0)
    local_spectra = spectra_of(stations, tables).reshape(stations.shape[0], N2 * 2 * KB)
    outgoing = jnp.where(
        present, jnp.take(local_spectra, chosen, axis=0), jnp.zeros((), jnp.bfloat16)
    )
    arrived = lax.all_to_all(outgoing, "pairs", split_axis=0, concat_axis=0, tiled=True)
    block_spectra = jnp.take(
        arrived.reshape(peer_count * slot_count, N2 * 2 * KB), arrival_rows, axis=0
    )
    block_spectra = block_spectra.reshape(block_width, N2, 2 * KB)
    partials = lag_partials(block_spectra[0], block_spectra[1:], tables)
    stacked = lax.psum_scatter(partials, "seg", scatter_dimension=2, tiled=True)
    segments = lax.axis_size("seg") * traces.shape[0]
    linear = stacked[0] / math.sqrt(segments)
    coherence = jnp.sqrt(stacked[1] * stacked[1] + stacked[2] * stacked[2]) / math.sqrt(segments)
    return linear * coherence


def solution(mesh):
    return jax.shard_map(
        local,
        mesh=mesh,
        in_specs=(P("seg", "pairs", None), P("pairs", None), P("pairs", None, None)),
        out_specs=P("pairs", "seg"),
        check_vma=False,
    )
```

profile of v0, /device:TPU:6, one launch (start us, length us, event | category | flops | bytes accessed | tf_op | source)
XLA Modules:
  0.0 215.4 jit_solution(17786327126377611632)
XLA Ops:
  6.5 2.0 negate_convert_fusion
  10.1 1.9 reshape_squeeze.3
  12.2 8.5 %while.12 = (s32[]{:T(128)}, bf16[2,2,300,64]{2,3,1,0:T(8,128)(2,1)S(1)}, bf16[2,2,72000]{2,1,0:T(2,128)(2,1)S(1)}, bf16[600,300]{0,1:T(8,128)(2,1)S(1)}, bf16[480,64]{0,1:T(8,128)(2,1)S(1)}, /*index=5*/s32[]{:T(128)}) while((s32[]{:T(128)}, bf16[2,2,300,64]{2,3,1,0:T(8,128)(2,1)S(1)}, ...), condition=%wide.region_3.4_spmd.clone.clone, body=%wide.region_1.3_spmd.clone.clone.sunk | while | flops 213057792 | bytes 7074189 | solution.py:76
  13.9 1.5 fusion.96
  18.1 1.5 fusion.96
  21.1 3.5 %gather_fusion = bf16[64,19200]{1,0:T(8,128)(2,1)} fusion(bf16[4,19200]{1,0:T(4,128)(2,1)S(1)} %reshape_reshape.3, s32[1024]{0:T(1024)S(1)} %pad_clamp_fusion.1), kind=kCustom, calls=%fused_computation | custom fusion | bytes 4915456 | tf_op jit(solution)/shard_map/jit(_take)/gather | solution.py:128
  24.7 2.0 fusion.25
  27.2 3.2 %reduce.2 = bf16[64,19200]{1,0:T(8,128)(2,1)} reduce(bf16[64,1,19200]{2,0,1:T(8,128)(2,1)S(1)} %fusion.25, bf16[]{:T(256)} %broadcast.295), dimensions={1}, to_apply=%copy.30.reduce_sub_computation | reduce | bytes 4915202 | tf_op jit(solution)/shard_map/jit(_where)/select_n | solution.py:127
  30.4 4.2 %reshape.310 = bf16[64,2,9600]{2,1,0:T(2,128)(2,1)} reshape(bf16[64,19200]{1,0:T(8,128)(2,1)} %reduce.2) | data formatting | bytes 4915200
  34.6 10.7 %all-to-all-start = ((bf16[64,2,9600]{2,1,0:T(2,128)(2,1)}), bf16[64,2,9600]{2,1,0:T(2,128)(2,1)S(1)}, u32[]{:S(2)}, u32[]{:S(2)}) async-start(bf16[64,2,9600]{2,1,0:T(2,128)(2,1)} %reshape.310), calls=%async_computation | async-start | bytes 4915200 | tf_op jit(solution)/shard_map/all_to_all | solution.py:130
  47.5 56.9 %all-to-all-done = bf16[64,2,9600]{2,1,0:T(2,128)(2,1)S(1)} async-done(((bf16[64,2,9600]{2,1,0:T(2,128)(2,1)}), bf16[64,2,9600]{2,1,0:T(2,128)(2,1)S(1)}, u32[]{:S(2)}, u32[]{:S(2)}) %all-to-all-start) | async-done | bytes 2457632 | tf_op jit(solution)/shard_map/all_to_all | solution.py:130
  104.4 6.8 %reshape.311 = bf16[64,1,19200]{2,1,0:T(2,128)(2,1)} reshape(bf16[64,2,9600]{2,1,0:T(2,128)(2,1)S(1)} %all-to-all-done) | data formatting | bytes 4915200
  111.2 2.7 %copy.45 = bf16[64,1,19200]{2,0,1:T(8,128)(2,1)S(1)} copy(bf16[64,1,19200]{2,1,0:T(2,128)(2,1)} %reshape.311) | data formatting | bytes 4915200
  113.8 2.3 %gather_fusion.1 = bf16[26,19200]{1,0:T(8,128)(2,1)} fusion(bf16[64,19200]{1,0:T(8,128)(2,1)S(1)} %bitcast.64, s32[1024]{0:T(1024)S(1)} %pad_clamp_fusion), kind=kCustom, calls=%fused_computation.1 | custom fusion | bytes 1996904 | tf_op jit(solution)/shard_map/jit(_take)/gather | solution.py:131
  118.1 3.0 %reshape.283 = f32[25,300,64]{2,1,0:T(8,128)} reshape(f32[25,19200]{1,0:T(8,128)S(1)} %slice_convert_fusion) | data formatting | bytes 3840000 | tf_op jit(solution)/shard_map/convert_element_type | solution.py:83
  121.1 7.6 %fusion.81 = (f32[25,300,32]{2,1,0:T(8,128)}, f32[25,300,32]{2,1,0:T(8,128)}) fusion(f32[25,300,64]{2,1,0:T(8,128)} %reshape.283), kind=kLoop, calls=%fused_computation.144 | loop fusion | bytes 3840000 | tf_op jit(solution)/shard_map/slice | solution.py:86
  128.7 3.2 %copy.39 = f32[25,300,32]{1,2,0:T(8,128)S(1)} copy(f32[25,300,32]{2,1,0:T(8,128)} %get-tuple-element.99) | data formatting | bytes 1920000
  131.8 3.2 %copy.40 = f32[25,300,32]{1,2,0:T(8,128)S(1)} copy(f32[25,300,32]{2,1,0:T(8,128)} %get-tuple-element.100) | data formatting | bytes 1920000
  137.3 2.2 %fusion.29 = f32[25,300,480]{2,1,0:T(8,128)S(1)} fusion(bf16[25,300,32]{1,2,0:T(8,128)(2,1)S(1)} %get-tuple-element.102, bf16[25,300,32]{1,2,0:T(8,128)(2,1)S(1)} %get-tuple-element.101, bf16[32,240]{1,0:T(8,128)(2,1)S(1)} %get-tuple-element.116, bf16[32,240]{1,0:T(8,128)(2,1)S(1)} %get-tuple-element.115, bf16[32,240]{1,0:T(8,128)(2,1)S(1)} %get-tuple-element.114), kind=kOutput, calls=%fused_computation.47 | convolution fusion | flops 462965760 | bytes 15406080 | tf_op jit(solution)/shard_map/pkf,fm->pkm/dot_general | solution.py:91
  139.5 3.7 %subtract_convert_fusion.1 = (bf16[25,300,240]{2,1,0:T(8,128)(2,1)S(1)}, bf16[25,300,240]{2,1,0:T(8,128)(2,1)S(1)}) fusion(f32[25,300,480]{2,1,0:T(8,128)S(1)} %fusion.29, f32[300,240]{1,0:T(8,128)S(1)} %get-tuple-element.125, f32[300,240]{1,0:T(8,128)S(1)} %get-tuple-element.124), kind=kLoop, calls=%fused_computation.40 | loop fusion | flops 14400000 | bytes 22176000 | tf_op jit(solution)/shard_map/convert.6
  143.2 2.6 %fusion.26 = f32[25,32,480]{2,1,0:T(8,128)S(1)} fusion(bf16[25,300,240]{2,1,0:T(8,128)(2,1)S(1)} %get-tuple-element.98, bf16[25,300,240]{2,1,0:T(8,128)(2,1)S(1)} %get-tuple-element.97, bf16[16,300]{1,0:T(8,128)(2,1)S(1)} %get-tuple-element.113, bf16[16,300]{1,0:T(8,128)(2,1)S(1)} %get-tuple-element.112), kind=kOutput, calls=%fused_computation.44 | convolution fusion | flops 244838400 | bytes 8755200 | tf_op jit(solution)/shard_map/jk,pkm->pjm/dot_general | solution.py:101
  147.0 5.0 %copy.36 = f32[3,25,3840]{1,0,2:T(4,128)} copy(f32[3,25,3840]{2,1,0:T(8,128)S(1)} %pad_maximum_fusion) | data formatting | bytes 2304000
  152.0 8.6 %reshape.307 = f32[3840,75]{1,0:T(8,128)} reshape(f32[3840,3,25]{2,1,0:T(4,128)} %bitcast.65) | data formatting | bytes 2304000
  160.7 44.9 %reduce-scatter.4.cloned.1.call-done = f32[480,75]{1,0:T(8,128)} async-done(((f32[3840,75]{1,0:T(8,128)}), f32[480,75]{1,0:T(8,128)}) %reduce-scatter.4.cloned.1.call-update) | async-done | bytes 144016
  (60 shorter events, 18.6 us)
Async XLA Ops:
  34.6 11.0 %copy-start = (s32[1,26]{1,0:T(1,128)S(1)}, s32[1,26]{1,0:T(1,128)}, u32[]{:S(2)}) copy-start(s32[1,26]{1,0:T(1,128)} %param.6) | copy-start | bytes 316
  34.6 69.8 %all-to-all-start = ((bf16[64,2,9600]{2,1,0:T(2,128)(2,1)}), bf16[64,2,9600]{2,1,0:T(2,128)(2,1)S(1)}, u32[]{:S(2)}, u32[]{:S(2)}) async-start(bf16[64,2,9600]{2,1,0:T(2,128)(2,1)} %reshape.310), calls=%async_computation | async-start | bytes 4915200 | tf_op jit(solution)/shard_map/all_to_all | solution.py:130
  45.3 160.2 %reduce-scatter.4.cloned.1.call-start = ((), (), s32[]{:S(2)}) async-start(), calls=%async_computation.2 | async-start | bytes 2211840
Sparse Core Ops, SparseCore 0:
  160.8 44.6 reduce-scatter.3
where the time goes:
time: 216 us; the launch traced here: 215 us
  waiting for transfers between devices  102 us (47%)
  local copies, waits for them, and re-layouts  59.9 us (28%)
  other arithmetic  22.7 us (11%)
  between operations  13.6 us (6%)
  starting transfers between devices  11 us (5%)
  matrix products  6.41 us (3%)
    all_to_all x1, waiting for transfers between devices, local(): lax.all_to_all(outgoing, 'pairs', split_axis=0, concat_axis=0, tiled=True)  56.9 us
    unnamed x2, waiting for transfers between devices  44.9 us
    unnamed x13, local copies, waits for them, and re-layouts  35.4 us
    all_to_all x1, starting transfers between devices, local(): lax.all_to_all(outgoing, 'pairs', split_axis=0, concat_axis=0, tiled=True)  10.7 us
    another operation x8, other arithmetic  7.57 us
    slice x1, local copies, waits for them, and re-layouts, lag_partials(): rec_real = receivers[..., :KB]  7.56 us
    select_n x2, other arithmetic, local(): jnp.where(present, jnp.take(local_spectra, chosen, axis=0), jnp.zeros((),...  5.23 us
  transfers between devices with their start and end apart: 2, of which 2 were waited for; matrix products, arithmetic and copies ran while one was open for 1% of the time, Pallas kernels for 0%

commit v1 on v0

v1 whole, which is shorter than its diff:
```python
import math

import jax
import jax.numpy as jnp
import numpy as np
from jax import lax
from jax.experimental import pallas as pl
from jax.experimental.pallas import tpu as pltpu
from jax.sharding import PartitionSpec as P

N1 = 240
N2 = 300
KB = 32
H = 8
ROWS = 152
HALF = 64
WIDE = 256
PAIRS = 25
LAGROWS = 56


def angles(left, right, period):
    product = (left[:, None] * right[None, :] % period).astype(np.float32)
    return product * np.float32(2.0 * math.pi / period)


def bf(table):
    return np.asarray(table, np.float32).astype(jnp.bfloat16)


def forward_tables():
    inner = np.arange(N2)
    outer = np.arange(N1)
    band = np.arange(1, KB + 1)
    a = angles(inner, inner, N2)
    dft = np.zeros((4 * ROWS, N2), np.float32)
    dft[:N2] = np.cos(a)
    dft[2 * ROWS : 2 * ROWS + N2] = -np.sin(a)
    t = angles(inner, outer, N1 * N2)
    twist = np.zeros((2, 2 * ROWS, N1), np.float32)
    twist[0, :N2] = np.cos(t)
    twist[1, :N2] = np.sin(t)
    o = angles(outer, band, N1)
    c, s = np.cos(o), np.sin(o)
    last = np.stack([np.concatenate([c, -s, c, -s], 1), np.concatenate([s, c, s, c], 1)])
    return bf(dft), bf(twist), bf(last)


def backward_tables():
    inner = np.arange(N2)
    outer = np.arange(N1)
    band = np.arange(1, KB + 1)
    o = angles(band, outer, N1)
    c, s = np.cos(o), np.sin(o)
    back = np.zeros((4 * HALF, 4 * WIDE), np.float32)
    for h in range(2):
        row, col = h * HALF, 2 * h * WIDE
        re, im = slice(col, col + N1), slice(col + WIDE, col + WIDE + N1)
        for at, to_re, to_im in (
            (row, c, s),
            (row + KB, s, -c),
            (2 * HALF + row, -s, c),
            (2 * HALF + row + KB, c, s),
        ):
            back[at : at + KB, re] = to_re
            back[at : at + KB, im] = to_im
    t = angles(inner, outer, N1 * N2)
    twist = np.zeros((2, 2, ROWS, WIDE), np.float32)
    for h in range(2):
        n = min(ROWS, N2 - h * ROWS)
        twist[h, 0, :n, :N1] = np.cos(t[h * ROWS : h * ROWS + n])
        twist[h, 1, :n, :N1] = np.sin(t[h * ROWS : h * ROWS + n])
    l = angles(np.arange(-H, H) % N2, inner, N2)
    lag = np.zeros((2, 4 * H, ROWS), np.float32)
    for h in range(2):
        n = min(ROWS, N2 - h * ROWS)
        lag[h, : 2 * H, :n] = np.cos(l[:, h * ROWS : h * ROWS + n])
        lag[h, 2 * H :, :n] = np.sin(l[:, h * ROWS : h * ROWS + n])
    return bf(back), bf(twist), bf(lag)


def spectrum_kernel(pick_ref, v_ref, dft_ref, twist_ref, last_ref, out_ref, held):
    cosine = twist_ref[0].astype(jnp.float32)
    sine = twist_ref[1].astype(jnp.float32)
    lane = lax.broadcasted_iota(jnp.int32, (ROWS, 2 * HALF), 1)
    for t in range(v_ref.shape[0]):
        y = jnp.dot(dft_ref[...], v_ref[t], preferred_element_type=jnp.float32)
        re, im = y[: 2 * ROWS], y[2 * ROWS :]
        a = (re * cosine + im * sine).astype(jnp.bfloat16)
        b = (im * cosine - re * sine).astype(jnp.bfloat16)
        x = jnp.dot(a, last_ref[0], preferred_element_type=jnp.float32)
        x = x + jnp.dot(b, last_ref[1], preferred_element_type=jnp.float32)
        power = x * x
        size = jnp.sqrt(power + pltpu.roll(power, KB, 1))
        level = jnp.sum(size, axis=0, keepdims=True) * (1.0 / N2) + 1e-6
        w = x * (1.0 / level)
        held[t] = jnp.where(lane < HALF, w[:ROWS], w[ROWS:]).astype(jnp.bfloat16)

    def send(b, carry):
        out_ref[b] = held[jnp.maximum(pick_ref[b], 0)]
        return carry

    lax.fori_loop(0, out_ref.shape[0], send, 0, unroll=4)


def spectrum_call(pick, v):
    dft, twist, last = forward_tables()
    slots = pick.shape[0]
    vmem = pl.BlockSpec(memory_space=pltpu.VMEM)
    return pl.pallas_call(
        spectrum_kernel,
        out_shape=jax.ShapeDtypeStruct((slots, ROWS, 2 * HALF), jnp.bfloat16),
        in_specs=[pl.BlockSpec(memory_space=pltpu.SMEM), vmem, vmem, vmem, vmem],
        out_specs=vmem,
        scratch_shapes=[pltpu.VMEM((v.shape[0], ROWS, 2 * HALF), jnp.bfloat16)],
        compiler_params=pltpu.CompilerParams(vmem_limit_bytes=48 * 2**20),
        name="spectrum",
    )(pick, v, jnp.asarray(dft), jnp.asarray(twist), jnp.asarray(last))


def lag_kernel(row_ref, w_ref, back_ref, twist_ref, lag_ref, out_ref, stage):
    lane = lax.broadcasted_iota(jnp.int32, (ROWS, 2 * HALF), 1) % HALF
    s = w_ref[row_ref[0]].astype(jnp.float32)
    s1 = jnp.where(lane < KB, s, pltpu.roll(s, KB, 1))
    s2 = jnp.where(lane < KB, pltpu.roll(s, 2 * HALF - KB, 1), s)
    stage[...] = jnp.zeros_like(stage)
    scale = 1.0 / math.sqrt(KB * N2)

    def pair(c, carry):
        r = w_ref[row_ref[c + 1]].astype(jnp.float32)
        both = jnp.concatenate([r * s1, r * s2], 1).astype(jnp.bfloat16)
        total = None
        for h in range(2):
            z = jnp.dot(
                both,
                back_ref[:, 2 * h * WIDE : 2 * (h + 1) * WIDE],
                preferred_element_type=jnp.float32,
            )
            re, im = z[:, :WIDE], z[:, WIDE:]
            cosine = twist_ref[h, 0].astype(jnp.float32)
            sine = twist_ref[h, 1].astype(jnp.float32)
            a = (re * cosine - im * sine).astype(jnp.bfloat16)
            b = (re * sine + im * cosine).astype(jnp.bfloat16)
            ab = jnp.concatenate([a, b], 1)
            part = jnp.dot(lag_ref[h], ab, preferred_element_type=jnp.float32)
            total = part if total is None else total + part
        re = (total[: 2 * H, :WIDE] - total[2 * H :, WIDE:]) * scale
        im = (total[2 * H :, :WIDE] + total[: 2 * H, WIDE:]) * scale
        both = jnp.concatenate([re, im], 1)
        for n in range(2 * H):
            stage[n // 2, pl.ds((n % 2) * PAIRS + c, 1)] = both[n : n + 1]
        return carry

    lax.fori_loop(0, PAIRS, pair, 0)
    out_ref[...] = stage[...].astype(jnp.bfloat16)


def lag_call(rows, w):
    back, twist, lag = backward_tables()
    vmem = pl.BlockSpec(memory_space=pltpu.VMEM)
    return pl.pallas_call(
        lag_kernel,
        out_shape=jax.ShapeDtypeStruct((H, LAGROWS, 2 * WIDE), jnp.bfloat16),
        in_specs=[pl.BlockSpec(memory_space=pltpu.SMEM), vmem, vmem, vmem, vmem],
        out_specs=vmem,
        scratch_shapes=[pltpu.VMEM((H, LAGROWS, 2 * WIDE), jnp.float32)],
        compiler_params=pltpu.CompilerParams(vmem_limit_bytes=48 * 2**20),
        name="lags",
    )(rows, w, jnp.asarray(back), jnp.asarray(twist), jnp.asarray(lag))


def stack_kernel(x_ref, out_ref):
    segments = x_ref.shape[0]
    linear = jnp.zeros((LAGROWS, WIDE), jnp.float32)
    phase_re = jnp.zeros((LAGROWS, WIDE), jnp.float32)
    phase_im = jnp.zeros((LAGROWS, WIDE), jnp.float32)
    for s in range(segments):
        re = x_ref[s, :, :WIDE].astype(jnp.float32)
        im = x_ref[s, :, WIDE:].astype(jnp.float32)
        inverse = 1.0 / jnp.maximum(jnp.sqrt(re * re + im * im), 0.25)
        linear = linear + re
        phase_re = phase_re + re * inverse
        phase_im = phase_im + im * inverse
    coherence = jnp.sqrt(phase_re * phase_re + phase_im * phase_im)
    pws = linear * coherence * (1.0 / segments)
    out_ref[:, :N1] = pws[:PAIRS, :N1]
    out_ref[:, N1:] = pws[PAIRS : 2 * PAIRS, :N1]


def stack_call(x):
    vmem = pl.BlockSpec(memory_space=pltpu.VMEM)
    return pl.pallas_call(
        stack_kernel,
        out_shape=jax.ShapeDtypeStruct((PAIRS, 2 * N1), jnp.float32),
        in_specs=[vmem],
        out_specs=vmem,
        compiler_params=pltpu.CompilerParams(vmem_limit_bytes=48 * 2**20),
        name="stack",
    )(x)


def local(traces, block_sources, send_lists):
    v = traces[0].reshape(traces.shape[1], N2, N1)
    pick = send_lists.reshape(-1)
    rows = block_sources.reshape(-1)
    outgoing = spectrum_call(pick, v)
    arrived = lax.all_to_all(outgoing, "pairs", split_axis=0, concat_axis=0, tiled=True)
    lags = lag_call(rows, arrived)
    lags = lax.all_to_all(lags, "seg", split_axis=0, concat_axis=0, tiled=True)
    return stack_call(lags)


def solution(mesh):
    return jax.shard_map(
        local,
        mesh=mesh,
        in_specs=(P("seg", "pairs", None), P("pairs", None), P("pairs", None, None)),
        out_specs=P("pairs", "seg"),
        check_vma=False,
    )
```

time: 216 us -> 121 us (0.56)
  waiting for transfers between devices: 102 us -> 0 us
  blocking collectives: 0 us -> 95.2 us
  local copies, waits for them, and re-layouts: 59.9 us -> 6.03 us
  other arithmetic: 22.7 us -> 0 us
  Pallas kernels: 0 us -> 17.5 us
  between operations: 13.6 us -> 0.08 us
  starting transfers between devices: 11 us -> 0 us
  matrix products: 6.41 us -> 0 us
    all_to_all x0 -> x2, blocking collectives: none -> 95.2 us  [the longest x1 70.2 us: local(): lax.all_to_all(outgoing, 'pairs', split_axis=0, concat_axis=0, tiled=True)]
    all_to_all x1 -> x0, waiting for transfers between devices: 56.9 us -> none  [local(): lax.all_to_all(outgoing, 'pairs', split_axis=0, concat_axis=0, tiled=True)]
    unnamed x2 -> x0, waiting for transfers between devices: 44.9 us -> none
    unnamed x13 -> x16, local copies, waits for them, and re-layouts: 35.4 us -> 3.57 us
    pallas_call x0 -> x3, Pallas kernels: none -> 17.5 us  [the longest x1 13.5 us: lag_call(): pl.pallas_call(lag_kernel, out_shape=jax.ShapeDtypeStruct((H, LAGROWS, 2...]
    all_to_all x1 -> x0, starting transfers between devices: 10.7 us -> none  [local(): lax.all_to_all(outgoing, 'pairs', split_axis=0, concat_axis=0, tiled=True)]
    slice x5 -> x0, local copies, waits for them, and re-layouts: 9.88 us -> none  [the longest x1 7.56 us: lag_partials(): rec_real = receivers[..., :KB]]
    another operation x9 -> x0, other arithmetic: 7.67 us -> none
  transfers between devices with their start and end apart: 2 -> 0, of which waited for: 2 -> 0; matrix products, arithmetic and copies ran while one was open for 1% -> 0% of each run, Pallas kernels for 0% -> 0%
where the time goes in v1:
time: 121 us; the launch traced here: 119 us
  blocking collectives  95.2 us (79%)
  Pallas kernels  17.5 us (14%)
  local copies, waits for them, and re-layouts  6.03 us (5%)
    all_to_all x1, blocking collectives, local(): lax.all_to_all(outgoing, 'pairs', split_axis=0, concat_axis=0, tiled=True)  70.2 us
    all_to_all x1, blocking collectives, local(): lags = lax.all_to_all(lags, 'seg', split_axis=0, concat_axis=0, tiled=True)  25 us
    pallas_call x1, Pallas kernels, lag_call(): pl.pallas_call(lag_kernel, out_shape=jax.ShapeDtypeStruct((H, LAGROWS, 2...  13.5 us
    unnamed x16, local copies, waits for them, and re-layouts  3.57 us
    pallas_call x1, Pallas kernels, spectrum_call(): pl.pallas_call(spectrum_kernel, out_shape=jax.ShapeDtypeStruct((slots, RO...  3 us
    another operation x1, local copies, waits for them, and re-layouts, local(): v = traces[0].reshape(traces.shape[1], N2, N1)  2.46 us

profile of v1, /device:TPU:6, one launch (start us, length us, event | category | flops | bytes accessed | tf_op | source)
XLA Modules:
  0.0 118.8 jit_solution(6907332141645050795)
XLA Ops:
  0.0 2.5 %reshape_squeeze.3.v_ref = bf16[4,300,240]{2,1,0:T(8,128)(2,1)S(1)} reshape(bf16[1,4,72000]{2,1,0:T(4,128)(2,1)} %param.9) | data formatting | bytes 1152000 | tf_op jit(solution)/shard_map/reshape;squeeze | solution.py:203
  2.5 0.0 copy-start.1
  2.5 1.0 copy-done.1
  3.5 0.0 copy-start.2
  3.5 1.0 copy-done.2
  4.5 0.0 copy-start.4
  4.5 0.9 copy-done.4
  5.4 0.0 copy-start.6
  5.4 0.7 copy-done.6
  6.0 3.0 %spectrum.1 = bf16[64,152,128]{2,1,0:T(8,128)(2,1)S(1)} custom-call(s32[64]{0:T(128)S(1)} %bitcast.2, bf16[4,300,240]{2,1,0:T(8,128)(2,1)S(1)} %reshape_squeeze.3.v_ref, bf16[608,300]{1,0:T(8,128)(2,1)S(1)} %copy-done.1, bf16[2,304,240]{2,1,0:T(8,128)(2,1)S(1)} %copy-done.2, bf16[2,240,128]{2,1,0:T(8,128)(2,1)S(1)} %copy-done.4), custom_call_target="tpu_custom_call" | custom-call | tf_op jit(solution)/shard_map/spectrum/pallas_call | solution.py:110
  9.0 0.0 copy-start
  9.0 0.0 copy-start.3
  9.1 0.0 copy-start.5
  9.1 0.0 copy-start.7
  9.1 70.2 %all_to_all.10.w_ref = bf16[64,152,128]{2,1,0:T(8,128)(2,1)S(1)} all-to-all(bf16[64,152,128]{2,1,0:T(8,128)(2,1)S(1)} %spectrum.1), channel_id=1, replica_groups=mesh['pairs'=64,'seg'=8] {'pairs'}, dimensions={0} | all-to-all | bytes 4980736 | tf_op jit(solution)/shard_map/all_to_all | solution.py:207
  79.3 0.0 copy-done
  79.3 0.0 copy-done.3
  79.3 0.0 copy-done.5
  79.3 0.0 copy-done.7
  79.3 13.5 %lags.1 = bf16[8,56,512]{2,1,0:T(8,128)(2,1)S(1)} custom-call(s32[26]{0:T(128)S(1)} %bitcast.3, bf16[64,152,128]{2,1,0:T(8,128)(2,1)S(1)} %all_to_all.10.w_ref, bf16[256,1024]{1,0:T(8,128)(2,1)S(1)} %copy-done, bf16[2,2,152,256]{3,2,1,0:T(8,128)(2,1)S(1)} %copy-done.3, bf16[2,32,152]{2,1,0:T(8,128)(2,1)S(1)} %copy-done.5), custom_call_target="tpu_custom_call" | custom-call | tf_op jit(solution)/shard_map/lags/pallas_call | solution.py:161
  92.9 25.0 %all_to_all.11.x_ref = bf16[8,56,512]{2,1,0:T(8,128)(2,1)S(1)} all-to-all(bf16[8,56,512]{2,1,0:T(8,128)(2,1)S(1)} %lags.1), channel_id=1, replica_groups=mesh['pairs'=64,'seg'=8] {'seg'}, dimensions={0} | all-to-all | bytes 917504 | tf_op jit(solution)/shard_map/all_to_all | solution.py:209
  117.9 0.9 stack.1
Async XLA Ops:
  2.5 1.0 copy-start.1
  3.5 1.0 copy-start.2
  4.5 0.9 copy-start.4
  5.4 0.7 copy-start.6
  9.0 70.3 %copy-start = (bf16[256,1024]{1,0:T(8,128)(2,1)S(1)}, bf16[256,1024]{1,0:T(8,128)(2,1)}, u32[]{:S(2)}) copy-start(bf16[256,1024]{1,0:T(8,128)(2,1)} %constant.15.clone.back_ref) | copy-start | bytes 1572868
  9.0 70.3 %copy-start.3 = (bf16[2,2,152,256]{3,2,1,0:T(8,128)(2,1)S(1)}, bf16[2,2,152,256]{3,2,1,0:T(8,128)(2,1)}, u32[]{:S(2)}) copy-start(bf16[2,2,152,256]{3,2,1,0:T(8,128)(2,1)} %constant.16.clone.twist_ref) | copy-start | bytes 933892
  9.1 70.3 %copy-start.5 = (bf16[2,32,152]{2,1,0:T(8,128)(2,1)S(1)}, bf16[2,32,152]{2,1,0:T(8,128)(2,1)}, u32[]{:S(2)}) copy-start(bf16[2,32,152]{2,1,0:T(8,128)(2,1)} %constant.17.clone.lag_ref) | copy-start | bytes 58372
  9.1 70.3 %copy-start.7 = (s32[1,26]{1,0:T(1,128)S(1)}, s32[1,26]{1,0:T(1,128)}, u32[]{:S(2)}) copy-start(s32[1,26]{1,0:T(1,128)} %param.10) | copy-start | bytes 316

commit v2 on v1

--- a/solution.py
+++ b/solution.py
@@ -16,6 +16,7 @@
 HALF = 64
 WIDE = 256
 PAIRS = 25
+GROUP = 25
 LAGROWS = 56
 
 
@@ -76,10 +77,28 @@
         n = min(ROWS, N2 - h * ROWS)
         lag[h, : 2 * H, :n] = np.cos(l[:, h * ROWS : h * ROWS + n])
         lag[h, 2 * H :, :n] = np.sin(l[:, h * ROWS : h * ROWS + n])
-    return bf(back), bf(twist), bf(lag)
-
-
-def spectrum_kernel(pick_ref, v_ref, dft_ref, twist_ref, last_ref, out_ref, held):
+    return bf(back), bf(twist).astype(np.float32), bf(lag)
+
+
+def spectrum_kernel(
+    pick_hbm, v_hbm, dft_hbm, twist_hbm, last_hbm, out_ref, held, pick_ref, v_ref, dft_ref, twist_ref, last_ref, sems
+):
+    copies = [
+        pltpu.make_async_copy(source, target, sems.at[i])
+        for i, (source, target) in enumerate(
+            (
+                (dft_hbm, dft_ref),
+                (twist_hbm, twist_ref),
+                (last_hbm, last_ref),
+                (v_hbm, v_ref),
+                (pick_hbm, pick_ref),
+            )
+        )
+    ]
+    for copy in copies:
+        copy.start()
+    for copy in copies:
+        copy.wait()
     cosine = twist_ref[0].astype(jnp.float32)
     sine = twist_ref[1].astype(jnp.float32)
     lane = lax.broadcasted_iota(jnp.int32, (ROWS, 2 * HALF), 1)
@@ -107,26 +126,34 @@
     dft, twist, last = forward_tables()
     slots = pick.shape[0]
     vmem = pl.BlockSpec(memory_space=pltpu.VMEM)
+    hbm = pl.BlockSpec(memory_space=pl.ANY)
     return pl.pallas_call(
         spectrum_kernel,
         out_shape=jax.ShapeDtypeStruct((slots, ROWS, 2 * HALF), jnp.bfloat16),
-        in_specs=[pl.BlockSpec(memory_space=pltpu.SMEM), vmem, vmem, vmem, vmem],
+        in_specs=[hbm, hbm, hbm, hbm, hbm],
         out_specs=vmem,
-        scratch_shapes=[pltpu.VMEM((v.shape[0], ROWS, 2 * HALF), jnp.bfloat16)],
-        compiler_params=pltpu.CompilerParams(vmem_limit_bytes=48 * 2**20),
+        scratch_shapes=[
+            pltpu.VMEM((v.shape[0], ROWS, 2 * HALF), jnp.bfloat16),
+            pltpu.SMEM((slots,), jnp.int32),
+            pltpu.VMEM(v.shape, jnp.bfloat16),
+            pltpu.VMEM(dft.shape, jnp.bfloat16),
+            pltpu.VMEM(twist.shape, jnp.bfloat16),
+            pltpu.VMEM(last.shape, jnp.bfloat16),
+            pltpu.SemaphoreType.DMA((5,)),
+        ],
+        compiler_params=pltpu.CompilerParams(vmem_limit_bytes=60 * 2**20),
         name="spectrum",
     )(pick, v, jnp.asarray(dft), jnp.asarray(twist), jnp.asarray(last))
 
 
-def lag_kernel(row_ref, w_ref, back_ref, twist_ref, lag_ref, out_ref, stage):
+def lag_kernel(row_ref, w_ref, back_ref, twist_ref, lag_ref, out_ref, stage, gather):
     lane = lax.broadcasted_iota(jnp.int32, (ROWS, 2 * HALF), 1) % HALF
     s = w_ref[row_ref[0]].astype(jnp.float32)
     s1 = jnp.where(lane < KB, s, pltpu.roll(s, KB, 1))
     s2 = jnp.where(lane < KB, pltpu.roll(s, 2 * HALF - KB, 1), s)
-    stage[...] = jnp.zeros_like(stage)
     scale = 1.0 / math.sqrt(KB * N2)
 
-    def pair(c, carry):
+    def pair(c):
         r = w_ref[row_ref[c + 1]].astype(jnp.float32)
         both = jnp.concatenate([r * s1, r * s2], 1).astype(jnp.bfloat16)
         total = None
@@ -137,8 +164,7 @@
                 preferred_element_type=jnp.float32,
             )
             re, im = z[:, :WIDE], z[:, WIDE:]
-            cosine = twist_ref[h, 0].astype(jnp.float32)
-            sine = twist_ref[h, 1].astype(jnp.float32)
+            cosine, sine = twist_ref[h, 0], twist_ref[h, 1]
             a = (re * cosine - im * sine).astype(jnp.bfloat16)
             b = (re * sine + im * cosine).astype(jnp.bfloat16)
             ab = jnp.concatenate([a, b], 1)
@@ -146,13 +172,24 @@
             total = part if total is None else total + part
         re = (total[: 2 * H, :WIDE] - total[2 * H :, WIDE:]) * scale
         im = (total[2 * H :, :WIDE] + total[: 2 * H, WIDE:]) * scale
-        both = jnp.concatenate([re, im], 1)
-        for n in range(2 * H):
-            stage[n // 2, pl.ds((n % 2) * PAIRS + c, 1)] = both[n : n + 1]
+        at = pl.ds(pl.multiple_of(c * 2 * H, 2 * H), 2 * H)
+        for lanes in range(2):
+            stage[lanes, at] = re[:, lanes * 128 : (lanes + 1) * 128]
+            stage[2 + lanes, at] = im[:, lanes * 128 : (lanes + 1) * 128]
+
+    def group(g, carry):
+        for i in range(GROUP):
+            pair(g * GROUP + i)
         return carry
 
-    lax.fori_loop(0, PAIRS, pair, 0)
-    out_ref[...] = stage[...].astype(jnp.bfloat16)
+    lax.fori_loop(0, PAIRS // GROUP, group, 0)
+    gather[...] = jnp.zeros_like(gather)
+    for j in range(H):
+        for n in range(2):
+            for lanes in range(4):
+                rows = stage.at[lanes][pl.ds(2 * j + n, PAIRS, stride=2 * H)]
+                gather[n * PAIRS : (n + 1) * PAIRS, lanes * 128 : (lanes + 1) * 128] = rows
+        out_ref[j] = gather[...].astype(jnp.bfloat16)
 
 
 def lag_call(rows, w):
@@ -163,7 +200,10 @@
         out_shape=jax.ShapeDtypeStruct((H, LAGROWS, 2 * WIDE), jnp.bfloat16),
         in_specs=[pl.BlockSpec(memory_space=pltpu.SMEM), vmem, vmem, vmem, vmem],
         out_specs=vmem,
-        scratch_shapes=[pltpu.VMEM((H, LAGROWS, 2 * WIDE), jnp.float32)],
+        scratch_shapes=[
+            pltpu.VMEM((4, PAIRS * 2 * H, 128), jnp.float32),
+            pltpu.VMEM((LAGROWS, 2 * WIDE), jnp.float32),
+        ],
         compiler_params=pltpu.CompilerParams(vmem_limit_bytes=48 * 2**20),
         name="lags",
     )(rows, w, jnp.asarray(back), jnp.asarray(twist), jnp.asarray(lag))

time: 121 us -> 115 us (0.950)
  Pallas kernels: 17.5 us -> 13.9 us
  local copies, waits for them, and re-layouts: 6.03 us -> 3.33 us
    pallas_call x1, Pallas kernels: 13.5 us -> 7.71 us  [lag_call(): pl.pallas_call(lag_kernel, out_shape=jax.ShapeDtypeStruct((H, LAGROWS, 2...]
    unnamed x16 -> x8, local copies, waits for them, and re-layouts: 3.57 us -> 0.03 us
    pallas_call x1, Pallas kernels: 3 us -> 5.29 us  [spectrum_call(): pl.pallas_call(spectrum_kernel, out_shape=jax.ShapeDtypeStruct((slots, RO...]
where the time goes in v2:
time: 115 us; the launch traced here: 113 us
  blocking collectives  95.5 us (83%)
  Pallas kernels  13.9 us (12%)
  local copies, waits for them, and re-layouts  3.33 us (3%)
    all_to_all x1, blocking collectives, local(): lax.all_to_all(outgoing, 'pairs', split_axis=0, concat_axis=0, tiled=True)  70.5 us
    all_to_all x1, blocking collectives, local(): lags = lax.all_to_all(lags, 'seg', split_axis=0, concat_axis=0, tiled=True)  25 us
    pallas_call x1, Pallas kernels, lag_call(): pl.pallas_call(lag_kernel, out_shape=jax.ShapeDtypeStruct((H, LAGROWS, 2...  7.71 us
    pallas_call x1, Pallas kernels, spectrum_call(): pl.pallas_call(spectrum_kernel, out_shape=jax.ShapeDtypeStruct((slots, RO...  5.29 us
    another operation x1, local copies, waits for them, and re-layouts, local(): v = traces[0].reshape(traces.shape[1], N2, N1)  3.3 us

profile of v2, /device:TPU:6, one launch (start us, length us, event | category | flops | bytes accessed | tf_op | source)
XLA Modules:
  0.0 112.8 jit_solution(16508788147023515828)
XLA Ops:
  0.0 3.3 %reshape_squeeze.3.v_hbm = bf16[4,300,240]{2,1,0:T(8,128)(2,1)} reshape(bf16[1,4,72000]{2,1,0:T(4,128)(2,1)} %param.9) | data formatting | bytes 1152000 | tf_op jit(solution)/shard_map/reshape;squeeze | solution.py:243
  3.3 5.3 %spectrum.1 = bf16[64,152,128]{2,1,0:T(8,128)(2,1)} custom-call(s32[64]{0:T(128)} %bitcast.3, bf16[4,300,240]{2,1,0:T(8,128)(2,1)} %reshape_squeeze.3.v_hbm, bf16[608,300]{1,0:T(8,128)(2,1)} %constant.12.clone.dft_hbm, bf16[2,304,240]{2,1,0:T(8,128)(2,1)} %constant.13.clone.twist_hbm, bf16[2,240,128]{2,1,0:T(8,128)(2,1)} %constant.14.clone.last_hbm), custom_call_target="tpu_custom_call" | custom-call | tf_op jit(solution)/shard_map/spectrum/pallas_call | solution.py:130
  8.6 0.0 copy-start
  8.6 0.0 copy-start.1
  8.6 0.0 copy-start.2
  8.6 0.0 copy-start.3
  8.7 70.5 %all_to_all.10.w_ref = bf16[64,152,128]{2,1,0:T(8,128)(2,1)S(1)} all-to-all(bf16[64,152,128]{2,1,0:T(8,128)(2,1)} %spectrum.1), channel_id=1, replica_groups=mesh['pairs'=64,'seg'=8] {'pairs'}, dimensions={0} | all-to-all | bytes 4980736 | tf_op jit(solution)/shard_map/all_to_all | solution.py:247
  79.1 0.0 copy-done
  79.1 0.0 copy-done.1
  79.1 0.0 copy-done.2
  79.1 0.0 copy-done.3
  79.1 7.7 %lags.1 = bf16[8,56,512]{2,1,0:T(8,128)(2,1)S(1)} custom-call(s32[26]{0:T(128)S(1)} %bitcast.2, bf16[64,152,128]{2,1,0:T(8,128)(2,1)S(1)} %all_to_all.10.w_ref, bf16[256,1024]{1,0:T(8,128)(2,1)S(1)} %copy-done.1, f32[2,2,152,256]{3,2,1,0:T(8,128)S(1)} %copy-done, bf16[2,32,152]{2,1,0:T(8,128)(2,1)S(1)} %copy-done.2), custom_call_target="tpu_custom_call" | custom-call | tf_op jit(solution)/shard_map/lags/pallas_call | solution.py:198
  86.8 25.0 %all_to_all.11.x_ref = bf16[8,56,512]{2,1,0:T(8,128)(2,1)S(1)} all-to-all(bf16[8,56,512]{2,1,0:T(8,128)(2,1)S(1)} %lags.1), channel_id=1, replica_groups=mesh['pairs'=64,'seg'=8] {'seg'}, dimensions={0} | all-to-all | bytes 917504 | tf_op jit(solution)/shard_map/all_to_all | solution.py:249
  111.9 0.9 stack.1
Async XLA Ops:
  8.6 70.5 %copy-start = (f32[2,2,152,256]{3,2,1,0:T(8,128)S(1)}, f32[2,2,152,256]{3,2,1,0:T(8,128)}, u32[]{:S(2)}) copy-start(f32[2,2,152,256]{3,2,1,0:T(8,128)} %constant.16.clone.twist_ref) | copy-start | bytes 1867780
  8.6 70.5 %copy-start.1 = (bf16[256,1024]{1,0:T(8,128)(2,1)S(1)}, bf16[256,1024]{1,0:T(8,128)(2,1)}, u32[]{:S(2)}) copy-start(bf16[256,1024]{1,0:T(8,128)(2,1)} %constant.15.clone.back_ref) | copy-start | bytes 1572868
  8.6 70.5 %copy-start.2 = (bf16[2,32,152]{2,1,0:T(8,128)(2,1)S(1)}, bf16[2,32,152]{2,1,0:T(8,128)(2,1)}, u32[]{:S(2)}) copy-start(bf16[2,32,152]{2,1,0:T(8,128)(2,1)} %constant.17.clone.lag_ref) | copy-start | bytes 58372
  8.6 70.5 %copy-start.3 = (s32[1,26]{1,0:T(1,128)S(1)}, s32[1,26]{1,0:T(1,128)}, u32[]{:S(2)}) copy-start(s32[1,26]{1,0:T(1,128)} %param.10) | copy-start | bytes 316

commit v3 on v2

--- a/solution.py
+++ b/solution.py
@@ -6,6 +6,7 @@
 from jax import lax
 from jax.experimental import pallas as pl
 from jax.experimental.pallas import tpu as pltpu
+from jax.sharding import Mesh
 from jax.sharding import PartitionSpec as P
 
 N1 = 240
@@ -18,6 +19,10 @@
 PAIRS = 25
 GROUP = 25
 LAGROWS = 56
+STATIONS = 4
+FAR = 4
+NEAR = 16
+TAIL = 148
 
 
 def angles(left, right, period):
@@ -81,7 +86,7 @@
 
 
 def spectrum_kernel(
-    pick_hbm, v_hbm, dft_hbm, twist_hbm, last_hbm, out_ref, held, pick_ref, v_ref, dft_ref, twist_ref, last_ref, sems
+    pick_hbm, v_hbm, dft_hbm, twist_hbm, last_hbm, out_ref, pick_ref, v_ref, dft_ref, twist_ref, last_ref, sems
 ):
     copies = [
         pltpu.make_async_copy(source, target, sems.at[i])
@@ -113,28 +118,28 @@
         size = jnp.sqrt(power + pltpu.roll(power, KB, 1))
         level = jnp.sum(size, axis=0, keepdims=True) * (1.0 / N2) + 1e-6
         w = x * (1.0 / level)
-        held[t] = jnp.where(lane < HALF, w[:ROWS], w[ROWS:]).astype(jnp.bfloat16)
-
-    def send(b, carry):
-        out_ref[b] = held[jnp.maximum(pick_ref[b], 0)]
-        return carry
-
-    lax.fori_loop(0, out_ref.shape[0], send, 0, unroll=4)
+        packed = jnp.where(lane < HALF, w[:ROWS], w[ROWS:])
+        row = lax.broadcasted_iota(jnp.int32, (8, 2 * HALF), 0) + (ROWS - 8)
+        upper = lax.broadcasted_iota(jnp.int32, (8, 2 * HALF), 1) >= HALF
+        for f in range(FAR):
+            tail = packed[ROWS - 8 :]
+            for i in range(NEAR // STATIONS):
+                wanted = pick_ref[f * NEAR + t * (NEAR // STATIONS) + i].astype(jnp.float32)
+                tail = jnp.where((row == TAIL + i) & upper, wanted, tail)
+            out_ref[f, t] = jnp.concatenate([packed[: ROWS - 8], tail], 0).astype(jnp.bfloat16)
 
 
 def spectrum_call(pick, v):
     dft, twist, last = forward_tables()
-    slots = pick.shape[0]
     vmem = pl.BlockSpec(memory_space=pltpu.VMEM)
     hbm = pl.BlockSpec(memory_space=pl.ANY)
     return pl.pallas_call(
         spectrum_kernel,
-        out_shape=jax.ShapeDtypeStruct((slots, ROWS, 2 * HALF), jnp.bfloat16),
+        out_shape=jax.ShapeDtypeStruct((FAR, STATIONS, ROWS, 2 * HALF), jnp.bfloat16),
         in_specs=[hbm, hbm, hbm, hbm, hbm],
         out_specs=vmem,
         scratch_shapes=[
-            pltpu.VMEM((v.shape[0], ROWS, 2 * HALF), jnp.bfloat16),
-            pltpu.SMEM((slots,), jnp.int32),
+            pltpu.SMEM(pick.shape, jnp.int32),
             pltpu.VMEM(v.shape, jnp.bfloat16),
             pltpu.VMEM(dft.shape, jnp.bfloat16),
             pltpu.VMEM(twist.shape, jnp.bfloat16),
@@ -146,15 +151,48 @@
     )(pick, v, jnp.asarray(dft), jnp.asarray(twist), jnp.asarray(last))
 
 
+def choose_kernel(x_ref, out_ref):
+    lane = lax.broadcasted_iota(jnp.int32, (8, 2 * HALF), 1)
+    for f in range(FAR):
+        for d in range(NEAR):
+            tail = x_ref[f, d // 4, ROWS - 16 :].astype(jnp.float32)[8:]
+            wanted = jnp.where(lane < HALF, pltpu.roll(tail, HALF, 1), tail)
+            wanted = wanted[TAIL - ROWS + 8 + d % 4 :][:1]
+            total = None
+            for t in range(STATIONS):
+                mask = jnp.where(wanted == t, 1.0, 0.0)
+                mask = jnp.broadcast_to(mask, (16, 2 * HALF)).astype(jnp.bfloat16)
+                mask = jnp.concatenate([mask] * 10, 0)[:ROWS]
+                part = x_ref[f, t] * mask
+                total = part if total is None else total + part
+            out_ref[d, f] = total
+
+
+def choose_call(x):
+    vmem = pl.BlockSpec(memory_space=pltpu.VMEM)
+    return pl.pallas_call(
+        choose_kernel,
+        out_shape=jax.ShapeDtypeStruct((NEAR, FAR, ROWS, 2 * HALF), jnp.bfloat16),
+        in_specs=[vmem],
+        out_specs=vmem,
+        compiler_params=pltpu.CompilerParams(vmem_limit_bytes=48 * 2**20),
+        name="choose",
+    )(x)
+
+
+def place(owner):
+    return (owner & (NEAR - 1)) * FAR + (owner >> 4)
+
+
 def lag_kernel(row_ref, w_ref, back_ref, twist_ref, lag_ref, out_ref, stage, gather):
     lane = lax.broadcasted_iota(jnp.int32, (ROWS, 2 * HALF), 1) % HALF
-    s = w_ref[row_ref[0]].astype(jnp.float32)
+    s = w_ref[place(row_ref[0])].astype(jnp.float32)
     s1 = jnp.where(lane < KB, s, pltpu.roll(s, KB, 1))
     s2 = jnp.where(lane < KB, pltpu.roll(s, 2 * HALF - KB, 1), s)
     scale = 1.0 / math.sqrt(KB * N2)
 
     def pair(c):
-        r = w_ref[row_ref[c + 1]].astype(jnp.float32)
+        r = w_ref[place(row_ref[c + 1])].astype(jnp.float32)
         both = jnp.concatenate([r * s1, r * s2], 1).astype(jnp.bfloat16)
         total = None
         for h in range(2):
@@ -240,21 +278,25 @@
 
 
 def local(traces, block_sources, send_lists):
-    v = traces[0].reshape(traces.shape[1], N2, N1)
+    v = traces[0].reshape(STATIONS, N2, N1)
     pick = send_lists.reshape(-1)
     rows = block_sources.reshape(-1)
-    outgoing = spectrum_call(pick, v)
-    arrived = lax.all_to_all(outgoing, "pairs", split_axis=0, concat_axis=0, tiled=True)
-    lags = lag_call(rows, arrived)
+    whitened = spectrum_call(pick, v)
+    whitened = lax.all_to_all(whitened, "far", split_axis=0, concat_axis=0, tiled=True)
+    chosen = choose_call(whitened)
+    chosen = lax.all_to_all(chosen, ("near", "cell"), split_axis=0, concat_axis=0, tiled=True)
+    lags = lag_call(rows, chosen.reshape(FAR * NEAR, ROWS, 2 * HALF))
     lags = lax.all_to_all(lags, "seg", split_axis=0, concat_axis=0, tiled=True)
     return stack_call(lags)
 
 
 def solution(mesh):
+    split = Mesh(mesh.devices.reshape(FAR, 2, NEAR // 2, -1), ("far", "near", "cell", "seg"))
+    pairs = ("far", "near", "cell")
     return jax.shard_map(
         local,
-        mesh=mesh,
-        in_specs=(P("seg", "pairs", None), P("pairs", None), P("pairs", None, None)),
-        out_specs=P("pairs", "seg"),
+        mesh=split,
+        in_specs=(P("seg", pairs, None), P(pairs, None), P(pairs, None, None)),
+        out_specs=P(pairs, "seg"),
         check_vma=False,
     )

time: 115 us -> 106 us (0.922)
  blocking collectives: 95.5 us -> 86.8 us
    all_to_all x1 -> x2, blocking collectives: 70.5 us -> 60.1 us  [the longest x1 34.5 us: local(): lax.all_to_all(chosen, ('near', 'cell'), split_axis=0, concat_axis=0, til...]
    all_to_all x1, blocking collectives: 25 us -> 26.7 us  [local(): lags = lax.all_to_all(lags, 'seg', split_axis=0, concat_axis=0, tiled=True)]
    pallas_call x1 -> x2, Pallas kernels: 5.29 us -> 6.02 us  [the longest x1 4.41 us: spectrum_call(): pl.pallas_call(spectrum_kernel, out_shape=jax.ShapeDtypeStruct((FAR, STAT...]
where the time goes in v3:
time: 106 us; the launch traced here: 105 us
  blocking collectives  86.8 us (82%)
  Pallas kernels  14.7 us (14%)
  local copies, waits for them, and re-layouts  3.33 us (3%)
    all_to_all x1, blocking collectives, local(): lax.all_to_all(chosen, ('near', 'cell'), split_axis=0, concat_axis=0, til...  34.5 us
    all_to_all x1, blocking collectives, local(): lags = lax.all_to_all(lags, 'seg', split_axis=0, concat_axis=0, tiled=True)  26.7 us
    all_to_all x1, blocking collectives, local(): lax.all_to_all(whitened, 'far', split_axis=0, concat_axis=0, tiled=True)  25.7 us
    pallas_call x1, Pallas kernels, lag_call(): pl.pallas_call(lag_kernel, out_shape=jax.ShapeDtypeStruct((H, LAGROWS, 2...  7.72 us
    pallas_call x1, Pallas kernels, spectrum_call(): pl.pallas_call(spectrum_kernel, out_shape=jax.ShapeDtypeStruct((FAR, STAT...  4.41 us
    another operation x1, local copies, waits for them, and re-layouts, local(): v = traces[0].reshape(STATIONS, N2, N1)  3.3 us

profile of v3, /device:TPU:6, one launch (start us, length us, event | category | flops | bytes accessed | tf_op | source)
XLA Modules:
  0.0 104.9 jit_solution(13364770084083921845)
XLA Ops:
  0.0 3.3 %reshape_squeeze.3.v_hbm = bf16[4,300,240]{2,1,0:T(8,128)(2,1)} reshape(bf16[1,4,72000]{2,1,0:T(4,128)(2,1)} %param.9) | data formatting | bytes 1152000 | tf_op jit(solution)/shard_map/reshape;squeeze | solution.py:281
  3.3 4.4 %spectrum.1 = bf16[4,4,152,128]{3,2,1,0:T(8,128)(2,1)} custom-call(s32[64]{0:T(128)} %bitcast.5, bf16[4,300,240]{2,1,0:T(8,128)(2,1)} %reshape_squeeze.3.v_hbm, bf16[608,300]{1,0:T(8,128)(2,1)} %constant.12.clone.dft_hbm, bf16[2,304,240]{2,1,0:T(8,128)(2,1)} %constant.13.clone.twist_hbm, bf16[2,240,128]{2,1,0:T(8,128)(2,1)} %constant.14.clone.last_hbm), custom_call_target="tpu_custom_call" | custom-call | tf_op jit(solution)/shard_map/spectrum/pallas_call | solution.py:136
  7.7 25.7 %all_to_all.15.x_ref = bf16[4,4,152,128]{3,2,1,0:T(8,128)(2,1)S(1)} all-to-all(bf16[4,4,152,128]{3,2,1,0:T(8,128)(2,1)} %spectrum.1), channel_id=1, replica_groups=mesh['far'=4,'near'=2,'cell'=8,'seg'=8] {'far'}, dimensions={0} | all-to-all | bytes 1245184 | tf_op jit(solution)/shard_map/all_to_all | solution.py:285
  33.4 1.6 %choose.1 = bf16[16,4,152,128]{3,2,1,0:T(8,128)(2,1)S(1)} custom-call(bf16[4,4,152,128]{3,2,1,0:T(8,128)(2,1)S(1)} %all_to_all.15.x_ref), custom_call_target="tpu_custom_call" | custom-call | tf_op jit(solution)/shard_map/choose/pallas_call | solution.py:173
  35.0 0.0 copy-start
  35.0 0.0 copy-start.1
  35.0 0.0 copy-start.2
  35.0 0.0 copy-start.3
  35.0 34.5 %all_to_all.16 = bf16[16,4,152,128]{3,2,1,0:T(8,128)(2,1)S(1)} all-to-all(bf16[16,4,152,128]{3,2,1,0:T(8,128)(2,1)S(1)} %choose.1), channel_id=1, replica_groups=mesh['far'=4,'near'=2,'cell'=8,'seg'=8] {'near','cell'}, dimensions={0} | all-to-all | bytes 4980736 | tf_op jit(solution)/shard_map/all_to_all | solution.py:287
  69.5 0.0 copy-done
  69.5 0.0 copy-done.1
  69.5 0.0 copy-done.2
  69.5 0.0 copy-done.3
  69.6 7.7 %lags.1 = bf16[8,56,512]{2,1,0:T(8,128)(2,1)S(1)} custom-call(s32[26]{0:T(128)S(1)} %bitcast.4, bf16[64,152,128]{2,1,0:T(8,128)(2,1)S(1)} %bitcast.3, bf16[256,1024]{1,0:T(8,128)(2,1)S(1)} %copy-done.1, f32[2,2,152,256]{3,2,1,0:T(8,128)S(1)} %copy-done, bf16[2,32,152]{2,1,0:T(8,128)(2,1)S(1)} %copy-done.2), custom_call_target="tpu_custom_call" | custom-call | tf_op jit(solution)/shard_map/lags/pallas_call | solution.py:236
  77.3 26.7 %all_to_all.17.x_ref = bf16[8,56,512]{2,1,0:T(8,128)(2,1)S(1)} all-to-all(bf16[8,56,512]{2,1,0:T(8,128)(2,1)S(1)} %lags.1), channel_id=1, replica_groups=mesh['far'=4,'near'=2,'cell'=8,'seg'=8] {'seg'}, dimensions={0} | all-to-all | bytes 917504 | tf_op jit(solution)/shard_map/all_to_all | solution.py:289
  103.9 0.9 stack.1
Async XLA Ops:
  35.0 34.5 %copy-start = (f32[2,2,152,256]{3,2,1,0:T(8,128)S(1)}, f32[2,2,152,256]{3,2,1,0:T(8,128)}, u32[]{:S(2)}) copy-start(f32[2,2,152,256]{3,2,1,0:T(8,128)} %constant.16.clone.twist_ref) | copy-start | bytes 1867780
  35.0 34.5 %copy-start.1 = (bf16[256,1024]{1,0:T(8,128)(2,1)S(1)}, bf16[256,1024]{1,0:T(8,128)(2,1)}, u32[]{:S(2)}) copy-start(bf16[256,1024]{1,0:T(8,128)(2,1)} %constant.15.clone.back_ref) | copy-start | bytes 1572868
  35.0 34.5 %copy-start.2 = (bf16[2,32,152]{2,1,0:T(8,128)(2,1)S(1)}, bf16[2,32,152]{2,1,0:T(8,128)(2,1)}, u32[]{:S(2)}) copy-start(bf16[2,32,152]{2,1,0:T(8,128)(2,1)} %constant.17.clone.lag_ref) | copy-start | bytes 58372
  35.0 34.5 %copy-start.3 = (s32[1,26]{1,0:T(1,128)S(1)}, s32[1,26]{1,0:T(1,128)}, u32[]{:S(2)}) copy-start(s32[1,26]{1,0:T(1,128)} %param.10) | copy-start | bytes 316

commit v4 on v3

--- a/solution.py
+++ b/solution.py
@@ -22,6 +22,10 @@
 STATIONS = 4
 FAR = 4
 NEAR = 16
+FOLD = 8
+STEP = FOLD * N1
+FULL = N2 // FOLD
+STAGED = 40
 TAIL = 148
 
 
@@ -39,9 +43,10 @@
     outer = np.arange(N1)
     band = np.arange(1, KB + 1)
     a = angles(inner, inner, N2)
-    dft = np.zeros((4 * ROWS, N2), np.float32)
-    dft[:N2] = np.cos(a)
-    dft[2 * ROWS : 2 * ROWS + N2] = -np.sin(a)
+    dft = np.zeros((4 * ROWS, FOLD * STAGED), np.float32)
+    column = inner % FOLD * STAGED + inner // FOLD
+    dft[:N2, column] = np.cos(a)
+    dft[2 * ROWS : 2 * ROWS + N2, column] = -np.sin(a)
     t = angles(inner, outer, N1 * N2)
     twist = np.zeros((2, 2 * ROWS, N1), np.float32)
     twist[0, :N2] = np.cos(t)
@@ -82,33 +87,47 @@
         n = min(ROWS, N2 - h * ROWS)
         lag[h, : 2 * H, :n] = np.cos(l[:, h * ROWS : h * ROWS + n])
         lag[h, 2 * H :, :n] = np.sin(l[:, h * ROWS : h * ROWS + n])
-    return bf(back), bf(twist).astype(np.float32), bf(lag)
+    return bf(back), bf(twist), bf(np.concatenate([lag[0], lag[1]], 1))
 
 
 def spectrum_kernel(
-    pick_hbm, v_hbm, dft_hbm, twist_hbm, last_hbm, out_ref, pick_ref, v_ref, dft_ref, twist_ref, last_ref, sems
+    pick_hbm, x_hbm, dft_hbm, twist_hbm, last_hbm, out_ref, pick_ref, x_ref, stage, dft_ref, twist_ref, last_ref, sems
 ):
     copies = [
         pltpu.make_async_copy(source, target, sems.at[i])
         for i, (source, target) in enumerate(
             (
+                (x_hbm, x_ref),
                 (dft_hbm, dft_ref),
                 (twist_hbm, twist_ref),
                 (last_hbm, last_ref),
-                (v_hbm, v_ref),
                 (pick_hbm, pick_ref),
             )
         )
     ]
     for copy in copies:
         copy.start()
-    for copy in copies:
+    tiles = STEP // 128
+    copies[0].wait()
+    stage[:, STAGED * STATIONS - 16 :] = jnp.zeros((tiles, 16, 128), jnp.float32)
+    for a in range(FULL):
+        chunk = x_ref[0, :, a * STEP : (a + 1) * STEP].astype(jnp.float32)
+        for c in range(tiles):
+            stage[c, a * STATIONS : (a + 1) * STATIONS] = chunk[:, c * 128 : (c + 1) * 128]
+    rest = x_ref[0, :, FULL * STEP :].astype(jnp.float32)
+    rest = jnp.concatenate([rest, jnp.zeros((STATIONS, STEP - rest.shape[1]), jnp.float32)], 1)
+    for c in range(tiles):
+        stage[c, FULL * STATIONS : (FULL + 1) * STATIONS] = rest[:, c * 128 : (c + 1) * 128]
+    for copy in copies[1:]:
         copy.wait()
     cosine = twist_ref[0].astype(jnp.float32)
     sine = twist_ref[1].astype(jnp.float32)
     lane = lax.broadcasted_iota(jnp.int32, (ROWS, 2 * HALF), 1)
-    for t in range(v_ref.shape[0]):
-        y = jnp.dot(dft_ref[...], v_ref[t], preferred_element_type=jnp.float32)
+    for t in range(STATIONS):
+        at = pl.ds(t, STAGED, stride=STATIONS)
+        rows = jnp.concatenate([stage.at[c][at] for c in range(tiles)], 1)
+        v = jnp.concatenate([rows[:, r * N1 : (r + 1) * N1] for r in range(FOLD)], 0)
+        y = jnp.dot(dft_ref[...], v.astype(jnp.bfloat16), preferred_element_type=jnp.float32)
         re, im = y[: 2 * ROWS], y[2 * ROWS :]
         a = (re * cosine + im * sine).astype(jnp.bfloat16)
         b = (im * cosine - re * sine).astype(jnp.bfloat16)
@@ -129,7 +148,7 @@
             out_ref[f, t] = jnp.concatenate([packed[: ROWS - 8], tail], 0).astype(jnp.bfloat16)
 
 
-def spectrum_call(pick, v):
+def spectrum_call(pick, x):
     dft, twist, last = forward_tables()
     vmem = pl.BlockSpec(memory_space=pltpu.VMEM)
     hbm = pl.BlockSpec(memory_space=pl.ANY)
@@ -140,7 +159,8 @@
         out_specs=vmem,
         scratch_shapes=[
             pltpu.SMEM(pick.shape, jnp.int32),
-            pltpu.VMEM(v.shape, jnp.bfloat16),
+            pltpu.VMEM(x.shape, jnp.bfloat16),
+            pltpu.VMEM((STEP // 128, STAGED * STATIONS, 128), jnp.float32),
             pltpu.VMEM(dft.shape, jnp.bfloat16),
             pltpu.VMEM(twist.shape, jnp.bfloat16),
             pltpu.VMEM(last.shape, jnp.bfloat16),
@@ -148,7 +168,7 @@
         ],
         compiler_params=pltpu.CompilerParams(vmem_limit_bytes=60 * 2**20),
         name="spectrum",
-    )(pick, v, jnp.asarray(dft), jnp.asarray(twist), jnp.asarray(last))
+    )(pick, x, jnp.asarray(dft), jnp.asarray(twist), jnp.asarray(last))
 
 
 def choose_kernel(x_ref, out_ref):
@@ -187,27 +207,27 @@
 def lag_kernel(row_ref, w_ref, back_ref, twist_ref, lag_ref, out_ref, stage, gather):
     lane = lax.broadcasted_iota(jnp.int32, (ROWS, 2 * HALF), 1) % HALF
     s = w_ref[place(row_ref[0])].astype(jnp.float32)
-    s1 = jnp.where(lane < KB, s, pltpu.roll(s, KB, 1))
-    s2 = jnp.where(lane < KB, pltpu.roll(s, 2 * HALF - KB, 1), s)
+    s1 = jnp.where(lane < KB, s, pltpu.roll(s, KB, 1)).astype(jnp.bfloat16)
+    s2 = jnp.where(lane < KB, pltpu.roll(s, 2 * HALF - KB, 1), s).astype(jnp.bfloat16)
     scale = 1.0 / math.sqrt(KB * N2)
 
     def pair(c):
-        r = w_ref[place(row_ref[c + 1])].astype(jnp.float32)
-        both = jnp.concatenate([r * s1, r * s2], 1).astype(jnp.bfloat16)
-        total = None
+        r = w_ref[place(row_ref[c + 1])]
+        both = jnp.concatenate([r * s1, r * s2], 1)
+        halves = []
         for h in range(2):
             z = jnp.dot(
                 both,
                 back_ref[:, 2 * h * WIDE : 2 * (h + 1) * WIDE],
                 preferred_element_type=jnp.float32,
             )
-            re, im = z[:, :WIDE], z[:, WIDE:]
+            re, im = z[:, :WIDE].astype(jnp.bfloat16), z[:, WIDE:].astype(jnp.bfloat16)
             cosine, sine = twist_ref[h, 0], twist_ref[h, 1]
-            a = (re * cosine - im * sine).astype(jnp.bfloat16)
-            b = (re * sine + im * cosine).astype(jnp.bfloat16)
+            a = re * cosine - im * sine
+            b = re * sine + im * cosine
             ab = jnp.concatenate([a, b], 1)
-            part = jnp.dot(lag_ref[h], ab, preferred_element_type=jnp.float32)
-            total = part if total is None else total + part
+            halves.append(ab)
+        total = jnp.dot(lag_ref[...], jnp.concatenate(halves, 0), preferred_element_type=jnp.float32)
         re = (total[: 2 * H, :WIDE] - total[2 * H :, WIDE:]) * scale
         im = (total[2 * H :, :WIDE] + total[: 2 * H, WIDE:]) * scale
         at = pl.ds(pl.multiple_of(c * 2 * H, 2 * H), 2 * H)
@@ -278,10 +298,9 @@
 
 
 def local(traces, block_sources, send_lists):
-    v = traces[0].reshape(STATIONS, N2, N1)
     pick = send_lists.reshape(-1)
     rows = block_sources.reshape(-1)
-    whitened = spectrum_call(pick, v)
+    whitened = spectrum_call(pick, traces)
     whitened = lax.all_to_all(whitened, "far", split_axis=0, concat_axis=0, tiled=True)
     chosen = choose_call(whitened)
     chosen = lax.all_to_all(chosen, ("near", "cell"), split_axis=0, concat_axis=0, tiled=True)

time: 106 us -> 102 us (0.962)
  local copies, waits for them, and re-layouts: 3.33 us -> 0.03 us
    another operation x1 -> x0, local copies, waits for them, and re-layouts: 3.3 us -> none  [local(): v = traces[0].reshape(STATIONS, N2, N1)]
where the time goes in v4:
time: 102 us; the launch traced here: 101 us
  blocking collectives  86.8 us (85%)
  Pallas kernels  14.1 us (14%)
    all_to_all x1, blocking collectives, local(): lax.all_to_all(chosen, ('near', 'cell'), split_axis=0, concat_axis=0, til...  34.5 us
    all_to_all x1, blocking collectives, local(): lags = lax.all_to_all(lags, 'seg', split_axis=0, concat_axis=0, tiled=True)  26.7 us
    all_to_all x1, blocking collectives, local(): lax.all_to_all(whitened, 'far', split_axis=0, concat_axis=0, tiled=True)  25.7 us
    pallas_call x1, Pallas kernels, lag_call(): pl.pallas_call(lag_kernel, out_shape=jax.ShapeDtypeStruct((H, LAGROWS, 2...  7.06 us
    pallas_call x1, Pallas kernels, spectrum_call(): pl.pallas_call(spectrum_kernel, out_shape=jax.ShapeDtypeStruct((FAR, STAT...  4.52 us

profile of v4, /device:TPU:6, one launch (start us, length us, event | category | flops | bytes accessed | tf_op | source)
XLA Modules:
  0.0 101.0 jit_solution(309926318117613664)
XLA Ops:
  0.0 4.5 %spectrum.1 = bf16[4,4,152,128]{3,2,1,0:T(8,128)(2,1)} custom-call(s32[64]{0:T(128)} %bitcast.5, bf16[1,4,72000]{2,1,0:T(4,128)(2,1)} %x_hbm.1, bf16[608,320]{1,0:T(8,128)(2,1)} %constant.12.clone.dft_hbm, bf16[2,304,240]{2,1,0:T(8,128)(2,1)} %constant.13.clone.twist_hbm, bf16[2,240,128]{2,1,0:T(8,128)(2,1)} %constant.14.clone.last_hbm), custom_call_target="tpu_custom_call" | custom-call | tf_op jit(solution)/shard_map/spectrum/pallas_call | solution.py:155
  4.5 25.7 %all_to_all.15.x_ref = bf16[4,4,152,128]{3,2,1,0:T(8,128)(2,1)S(1)} all-to-all(bf16[4,4,152,128]{3,2,1,0:T(8,128)(2,1)} %spectrum.1), channel_id=1, replica_groups=mesh['far'=4,'near'=2,'cell'=8,'seg'=8] {'far'}, dimensions={0} | all-to-all | bytes 1245184 | tf_op jit(solution)/shard_map/all_to_all | solution.py:304
  30.2 1.6 %choose.1 = bf16[16,4,152,128]{3,2,1,0:T(8,128)(2,1)S(1)} custom-call(bf16[4,4,152,128]{3,2,1,0:T(8,128)(2,1)S(1)} %all_to_all.15.x_ref), custom_call_target="tpu_custom_call" | custom-call | tf_op jit(solution)/shard_map/choose/pallas_call | solution.py:193
  31.8 0.0 copy-start
  31.8 0.0 copy-start.1
  31.8 0.0 copy-start.2
  31.8 0.0 copy-start.3
  31.9 34.5 %all_to_all.16 = bf16[16,4,152,128]{3,2,1,0:T(8,128)(2,1)S(1)} all-to-all(bf16[16,4,152,128]{3,2,1,0:T(8,128)(2,1)S(1)} %choose.1), channel_id=1, replica_groups=mesh['far'=4,'near'=2,'cell'=8,'seg'=8] {'near','cell'}, dimensions={0} | all-to-all | bytes 4980736 | tf_op jit(solution)/shard_map/all_to_all | solution.py:306
  66.3 0.0 copy-done
  66.3 0.0 copy-done.1
  66.3 0.0 copy-done.2
  66.3 0.0 copy-done.3
  66.4 7.1 %lags.1 = bf16[8,56,512]{2,1,0:T(8,128)(2,1)S(1)} custom-call(s32[26]{0:T(128)S(1)} %bitcast.4, bf16[64,152,128]{2,1,0:T(8,128)(2,1)S(1)} %bitcast.3, bf16[256,1024]{1,0:T(8,128)(2,1)S(1)} %copy-done, bf16[2,2,152,256]{3,2,1,0:T(8,128)(2,1)S(1)} %copy-done.1, bf16[32,304]{1,0:T(8,128)(2,1)S(1)} %copy-done.2), custom_call_target="tpu_custom_call" | custom-call | tf_op jit(solution)/shard_map/lags/pallas_call | solution.py:256
  73.4 26.7 %all_to_all.17.x_ref = bf16[8,56,512]{2,1,0:T(8,128)(2,1)S(1)} all-to-all(bf16[8,56,512]{2,1,0:T(8,128)(2,1)S(1)} %lags.1), channel_id=1, replica_groups=mesh['far'=4,'near'=2,'cell'=8,'seg'=8] {'seg'}, dimensions={0} | all-to-all | bytes 917504 | tf_op jit(solution)/shard_map/all_to_all | solution.py:308
  100.1 0.9 stack.1
Async XLA Ops:
  31.8 34.5 %copy-start = (bf16[256,1024]{1,0:T(8,128)(2,1)S(1)}, bf16[256,1024]{1,0:T(8,128)(2,1)}, u32[]{:S(2)}) copy-start(bf16[256,1024]{1,0:T(8,128)(2,1)} %constant.15.clone.back_ref) | copy-start | bytes 1572868
  31.8 34.5 %copy-start.1 = (bf16[2,2,152,256]{3,2,1,0:T(8,128)(2,1)S(1)}, bf16[2,2,152,256]{3,2,1,0:T(8,128)(2,1)}, u32[]{:S(2)}) copy-start(bf16[2,2,152,256]{3,2,1,0:T(8,128)(2,1)} %constant.16.clone.twist_ref) | copy-start | bytes 933892
  31.8 34.5 %copy-start.2 = (bf16[32,304]{1,0:T(8,128)(2,1)S(1)}, bf16[32,304]{1,0:T(8,128)(2,1)}, u32[]{:S(2)}) copy-start(bf16[32,304]{1,0:T(8,128)(2,1)} %constant.17.clone.lag_ref) | copy-start | bytes 58372
  31.8 34.5 %copy-start.3 = (s32[1,26]{1,0:T(1,128)S(1)}, s32[1,26]{1,0:T(1,128)}, u32[]{:S(2)}) copy-start(s32[1,26]{1,0:T(1,128)} %param.10) | copy-start | bytes 316

commit v5 on v4

--- a/solution.py
+++ b/solution.py
@@ -17,7 +17,7 @@
 HALF = 64
 WIDE = 256
 PAIRS = 25
-GROUP = 25
+PITCH = 160
 LAGROWS = 56
 STATIONS = 4
 FAR = 4
@@ -174,18 +174,20 @@
 def choose_kernel(x_ref, out_ref):
     lane = lax.broadcasted_iota(jnp.int32, (8, 2 * HALF), 1)
     for f in range(FAR):
+        wanted = []
         for d in range(NEAR):
-            tail = x_ref[f, d // 4, ROWS - 16 :].astype(jnp.float32)[8:]
-            wanted = jnp.where(lane < HALF, pltpu.roll(tail, HALF, 1), tail)
-            wanted = wanted[TAIL - ROWS + 8 + d % 4 :][:1]
-            total = None
-            for t in range(STATIONS):
-                mask = jnp.where(wanted == t, 1.0, 0.0)
-                mask = jnp.broadcast_to(mask, (16, 2 * HALF)).astype(jnp.bfloat16)
-                mask = jnp.concatenate([mask] * 10, 0)[:ROWS]
-                part = x_ref[f, t] * mask
-                total = part if total is None else total + part
-            out_ref[d, f] = total
+            tail = x_ref[f, d // 4, ROWS - 8 :].astype(jnp.float32)
+            tail = jnp.where(lane < HALF, pltpu.roll(tail, HALF, 1), tail)
+            row = TAIL - ROWS + 8 + d % 4
+            wanted.append(jnp.broadcast_to(tail[row : row + 1], (16, 2 * HALF)).astype(jnp.bfloat16))
+        for k in range(0, ROWS, 16):
+            n = min(16, ROWS - k)
+            parts = [x_ref[f, t, k : k + n] for t in range(STATIONS)]
+            for d in range(NEAR):
+                best = parts[0]
+                for t in range(1, STATIONS):
+                    best = jnp.where(wanted[d][:n] == t, parts[t], best)
+                out_ref[d, f, k : k + n] = best
 
 
 def choose_call(x):
@@ -204,43 +206,44 @@
     return (owner & (NEAR - 1)) * FAR + (owner >> 4)
 
 
-def lag_kernel(row_ref, w_ref, back_ref, twist_ref, lag_ref, out_ref, stage, gather):
+def lag_kernel(row_ref, w_ref, back_ref, twist_ref, lag_ref, out_ref, stage, gather, product):
     lane = lax.broadcasted_iota(jnp.int32, (ROWS, 2 * HALF), 1) % HALF
     s = w_ref[place(row_ref[0])].astype(jnp.float32)
     s1 = jnp.where(lane < KB, s, pltpu.roll(s, KB, 1)).astype(jnp.bfloat16)
     s2 = jnp.where(lane < KB, pltpu.roll(s, 2 * HALF - KB, 1), s).astype(jnp.bfloat16)
     scale = 1.0 / math.sqrt(KB * N2)
 
-    def pair(c):
-        r = w_ref[place(row_ref[c + 1])]
-        both = jnp.concatenate([r * s1, r * s2], 1)
-        halves = []
-        for h in range(2):
-            z = jnp.dot(
-                both,
-                back_ref[:, 2 * h * WIDE : 2 * (h + 1) * WIDE],
-                preferred_element_type=jnp.float32,
-            )
-            re, im = z[:, :WIDE].astype(jnp.bfloat16), z[:, WIDE:].astype(jnp.bfloat16)
-            cosine, sine = twist_ref[h, 0], twist_ref[h, 1]
+    for i in range(PAIRS):
+        r = w_ref[place(row_ref[i + 1])]
+        product[i, :ROWS] = jnp.concatenate([r * s1, r * s2], 1)
+    both = product[...].reshape(PAIRS * PITCH, 4 * HALF)
+    turned = [[] for _ in range(PAIRS)]
+    for h in range(2):
+        z = jnp.dot(
+            both,
+            back_ref[:, 2 * h * WIDE : 2 * (h + 1) * WIDE],
+            preferred_element_type=jnp.float32,
+        ).astype(jnp.bfloat16)
+        cosine, sine = twist_ref[h, 0], twist_ref[h, 1]
+        for i in range(PAIRS):
+            mine = z[i * PITCH : i * PITCH + ROWS]
+            re, im = mine[:, :WIDE], mine[:, WIDE:]
             a = re * cosine - im * sine
             b = re * sine + im * cosine
-            ab = jnp.concatenate([a, b], 1)
-            halves.append(ab)
-        total = jnp.dot(lag_ref[...], jnp.concatenate(halves, 0), preferred_element_type=jnp.float32)
+            turned[i].append(jnp.concatenate([a, b], 1))
+    for i in range(PAIRS):
+        total = jnp.dot(
+            lag_ref[...],
+            jnp.concatenate(turned[i], 0),
+            preferred_element_type=jnp.float32,
+        )
         re = (total[: 2 * H, :WIDE] - total[2 * H :, WIDE:]) * scale
         im = (total[2 * H :, :WIDE] + total[: 2 * H, WIDE:]) * scale
-        at = pl.ds(pl.multiple_of(c * 2 * H, 2 * H), 2 * H)
+        at = pl.ds(i * 2 * H, 2 * H)
         for lanes in range(2):
             stage[lanes, at] = re[:, lanes * 128 : (lanes + 1) * 128]
             stage[2 + lanes, at] = im[:, lanes * 128 : (lanes + 1) * 128]
 
-    def group(g, carry):
-        for i in range(GROUP):
-            pair(g * GROUP + i)
-        return carry
-
-    lax.fori_loop(0, PAIRS // GROUP, group, 0)
     gather[...] = jnp.zeros_like(gather)
     for j in range(H):
         for n in range(2):
@@ -261,6 +264,7 @@
         scratch_shapes=[
             pltpu.VMEM((4, PAIRS * 2 * H, 128), jnp.float32),
             pltpu.VMEM((LAGROWS, 2 * WIDE), jnp.float32),
+            pltpu.VMEM((PAIRS, PITCH, 4 * HALF), jnp.bfloat16),
         ],
         compiler_params=pltpu.CompilerParams(vmem_limit_bytes=48 * 2**20),
         name="lags",

time: 102 us -> 98.1 us (0.962)
  Pallas kernels: 14.1 us -> 10.6 us
    pallas_call x1, Pallas kernels: 7.06 us -> 4.53 us  [lag_call(): pl.pallas_call(lag_kernel, out_shape=jax.ShapeDtypeStruct((H, LAGROWS, 2...]
where the time goes in v5:
time: 98.1 us; the launch traced here: 97.5 us
  blocking collectives  86.8 us (88%)
  Pallas kernels  10.6 us (11%)
    all_to_all x1, blocking collectives, local(): lax.all_to_all(chosen, ('near', 'cell'), split_axis=0, concat_axis=0, til...  34.5 us
    all_to_all x1, blocking collectives, local(): lags = lax.all_to_all(lags, 'seg', split_axis=0, concat_axis=0, tiled=True)  26.6 us
    all_to_all x1, blocking collectives, local(): lax.all_to_all(whitened, 'far', split_axis=0, concat_axis=0, tiled=True)  25.7 us
    pallas_call x1, Pallas kernels, lag_call(): pl.pallas_call(lag_kernel, out_shape=jax.ShapeDtypeStruct((H, LAGROWS, 2...  4.53 us
    pallas_call x1, Pallas kernels, spectrum_call(): pl.pallas_call(spectrum_kernel, out_shape=jax.ShapeDtypeStruct((FAR, STAT...  4.52 us

profile of v5, /device:TPU:6, one launch (start us, length us, event | category | flops | bytes accessed | tf_op | source)
XLA Modules:
  0.0 97.5 jit_solution(9608224236924082640)
XLA Ops:
  0.0 4.5 %spectrum.1 = bf16[4,4,152,128]{3,2,1,0:T(8,128)(2,1)} custom-call(s32[64]{0:T(128)} %bitcast.5, bf16[1,4,72000]{2,1,0:T(4,128)(2,1)} %x_hbm.1, bf16[608,320]{1,0:T(8,128)(2,1)} %constant.12.clone.dft_hbm, bf16[2,304,240]{2,1,0:T(8,128)(2,1)} %constant.13.clone.twist_hbm, bf16[2,240,128]{2,1,0:T(8,128)(2,1)} %constant.14.clone.last_hbm), custom_call_target="tpu_custom_call" | custom-call | tf_op jit(solution)/shard_map/spectrum/pallas_call | solution.py:155
  4.5 25.7 %all_to_all.15.x_ref = bf16[4,4,152,128]{3,2,1,0:T(8,128)(2,1)S(1)} all-to-all(bf16[4,4,152,128]{3,2,1,0:T(8,128)(2,1)} %spectrum.1), channel_id=1, replica_groups=mesh['far'=4,'near'=2,'cell'=8,'seg'=8] {'far'}, dimensions={0} | all-to-all | bytes 1245184 | tf_op jit(solution)/shard_map/all_to_all | solution.py:308
  30.2 0.6 choose.1
  30.8 0.0 copy-start
  30.8 0.0 copy-start.1
  30.8 0.0 copy-start.2
  30.8 0.0 copy-start.3
  30.8 34.5 %all_to_all.16 = bf16[16,4,152,128]{3,2,1,0:T(8,128)(2,1)S(1)} all-to-all(bf16[16,4,152,128]{3,2,1,0:T(8,128)(2,1)S(1)} %choose.1), channel_id=1, replica_groups=mesh['far'=4,'near'=2,'cell'=8,'seg'=8] {'near','cell'}, dimensions={0} | all-to-all | bytes 4980736 | tf_op jit(solution)/shard_map/all_to_all | solution.py:310
  65.3 0.0 copy-done
  65.3 0.0 copy-done.1
  65.3 0.0 copy-done.2
  65.3 0.0 copy-done.3
  65.3 4.5 %lags.1 = bf16[8,56,512]{2,1,0:T(8,128)(2,1)S(1)} custom-call(s32[26]{0:T(128)S(1)} %bitcast.4, bf16[64,152,128]{2,1,0:T(8,128)(2,1)S(1)} %bitcast.3, bf16[256,1024]{1,0:T(8,128)(2,1)S(1)} %copy-done, bf16[2,2,152,256]{3,2,1,0:T(8,128)(2,1)S(1)} %copy-done.1, bf16[32,304]{1,0:T(8,128)(2,1)S(1)} %copy-done.2), custom_call_target="tpu_custom_call" | custom-call | tf_op jit(solution)/shard_map/lags/pallas_call | solution.py:259
  69.9 26.6 %all_to_all.17.x_ref = bf16[8,56,512]{2,1,0:T(8,128)(2,1)S(1)} all-to-all(bf16[8,56,512]{2,1,0:T(8,128)(2,1)S(1)} %lags.1), channel_id=1, replica_groups=mesh['far'=4,'near'=2,'cell'=8,'seg'=8] {'seg'}, dimensions={0} | all-to-all | bytes 917504 | tf_op jit(solution)/shard_map/all_to_all | solution.py:312
  96.5 0.9 stack.1
Async XLA Ops:
  30.8 34.5 %copy-start = (bf16[256,1024]{1,0:T(8,128)(2,1)S(1)}, bf16[256,1024]{1,0:T(8,128)(2,1)}, u32[]{:S(2)}) copy-start(bf16[256,1024]{1,0:T(8,128)(2,1)} %constant.15.clone.back_ref) | copy-start | bytes 1572868
  30.8 34.5 %copy-start.1 = (bf16[2,2,152,256]{3,2,1,0:T(8,128)(2,1)S(1)}, bf16[2,2,152,256]{3,2,1,0:T(8,128)(2,1)}, u32[]{:S(2)}) copy-start(bf16[2,2,152,256]{3,2,1,0:T(8,128)(2,1)} %constant.16.clone.twist_ref) | copy-start | bytes 933892
  30.8 34.5 %copy-start.2 = (bf16[32,304]{1,0:T(8,128)(2,1)S(1)}, bf16[32,304]{1,0:T(8,128)(2,1)}, u32[]{:S(2)}) copy-start(bf16[32,304]{1,0:T(8,128)(2,1)} %constant.17.clone.lag_ref) | copy-start | bytes 58372
  30.8 34.5 %copy-start.3 = (s32[1,26]{1,0:T(1,128)S(1)}, s32[1,26]{1,0:T(1,128)}, u32[]{:S(2)}) copy-start(s32[1,26]{1,0:T(1,128)} %param.10) | copy-start | bytes 316

commit v6 on v5

--- a/solution.py
+++ b/solution.py
@@ -18,7 +18,7 @@
 WIDE = 256
 PAIRS = 25
 PITCH = 160
-LAGROWS = 56
+LAGROWS = 8 * PAIRS
 STATIONS = 4
 FAR = 4
 NEAR = 16
@@ -123,23 +123,26 @@
     cosine = twist_ref[0].astype(jnp.float32)
     sine = twist_ref[1].astype(jnp.float32)
     lane = lax.broadcasted_iota(jnp.int32, (ROWS, 2 * HALF), 1)
+    reals, imags = [], []
     for t in range(STATIONS):
         at = pl.ds(t, STAGED, stride=STATIONS)
         rows = jnp.concatenate([stage.at[c][at] for c in range(tiles)], 1)
         v = jnp.concatenate([rows[:, r * N1 : (r + 1) * N1] for r in range(FOLD)], 0)
         y = jnp.dot(dft_ref[...], v.astype(jnp.bfloat16), preferred_element_type=jnp.float32)
         re, im = y[: 2 * ROWS], y[2 * ROWS :]
-        a = (re * cosine + im * sine).astype(jnp.bfloat16)
-        b = (im * cosine - re * sine).astype(jnp.bfloat16)
-        x = jnp.dot(a, last_ref[0], preferred_element_type=jnp.float32)
-        x = x + jnp.dot(b, last_ref[1], preferred_element_type=jnp.float32)
+        reals.append((re * cosine + im * sine).astype(jnp.bfloat16))
+        imags.append((im * cosine - re * sine).astype(jnp.bfloat16))
+    spectra = jnp.dot(jnp.concatenate(reals, 0), last_ref[0], preferred_element_type=jnp.float32)
+    spectra = spectra + jnp.dot(jnp.concatenate(imags, 0), last_ref[1], preferred_element_type=jnp.float32)
+    row = lax.broadcasted_iota(jnp.int32, (8, 2 * HALF), 0) + (ROWS - 8)
+    upper = lax.broadcasted_iota(jnp.int32, (8, 2 * HALF), 1) >= HALF
+    for t in range(STATIONS):
+        x = spectra[2 * ROWS * t : 2 * ROWS * (t + 1)]
         power = x * x
         size = jnp.sqrt(power + pltpu.roll(power, KB, 1))
         level = jnp.sum(size, axis=0, keepdims=True) * (1.0 / N2) + 1e-6
         w = x * (1.0 / level)
         packed = jnp.where(lane < HALF, w[:ROWS], w[ROWS:])
-        row = lax.broadcasted_iota(jnp.int32, (8, 2 * HALF), 0) + (ROWS - 8)
-        upper = lax.broadcasted_iota(jnp.int32, (8, 2 * HALF), 1) >= HALF
         for f in range(FAR):
             tail = packed[ROWS - 8 :]
             for i in range(NEAR // STATIONS):
@@ -244,12 +247,11 @@
             stage[lanes, at] = re[:, lanes * 128 : (lanes + 1) * 128]
             stage[2 + lanes, at] = im[:, lanes * 128 : (lanes + 1) * 128]
 
-    gather[...] = jnp.zeros_like(gather)
     for j in range(H):
-        for n in range(2):
-            for lanes in range(4):
+        for lanes in range(4):
+            for n in range(2):
                 rows = stage.at[lanes][pl.ds(2 * j + n, PAIRS, stride=2 * H)]
-                gather[n * PAIRS : (n + 1) * PAIRS, lanes * 128 : (lanes + 1) * 128] = rows
+                gather[pl.ds((2 * lanes + n) * PAIRS, PAIRS)] = rows
         out_ref[j] = gather[...].astype(jnp.bfloat16)
 
 
@@ -258,12 +260,12 @@
     vmem = pl.BlockSpec(memory_space=pltpu.VMEM)
     return pl.pallas_call(
         lag_kernel,
-        out_shape=jax.ShapeDtypeStruct((H, LAGROWS, 2 * WIDE), jnp.bfloat16),
+        out_shape=jax.ShapeDtypeStruct((H, LAGROWS, 128), jnp.bfloat16),
         in_specs=[pl.BlockSpec(memory_space=pltpu.SMEM), vmem, vmem, vmem, vmem],
         out_specs=vmem,
         scratch_shapes=[
             pltpu.VMEM((4, PAIRS * 2 * H, 128), jnp.float32),
-            pltpu.VMEM((LAGROWS, 2 * WIDE), jnp.float32),
+            pltpu.VMEM((LAGROWS, 128), jnp.float32),
             pltpu.VMEM((PAIRS, PITCH, 4 * HALF), jnp.bfloat16),
         ],
         compiler_params=pltpu.CompilerParams(vmem_limit_bytes=48 * 2**20),
@@ -273,20 +275,24 @@
 
 def stack_kernel(x_ref, out_ref):
     segments = x_ref.shape[0]
-    linear = jnp.zeros((LAGROWS, WIDE), jnp.float32)
-    phase_re = jnp.zeros((LAGROWS, WIDE), jnp.float32)
-    phase_im = jnp.zeros((LAGROWS, WIDE), jnp.float32)
+    half = LAGROWS // 2
+    linear = phase_re = phase_im = None
     for s in range(segments):
-        re = x_ref[s, :, :WIDE].astype(jnp.float32)
-        im = x_ref[s, :, WIDE:].astype(jnp.float32)
+        x = x_ref[s].astype(jnp.float32)
+        re, im = x[:half], x[half:]
         inverse = 1.0 / jnp.maximum(jnp.sqrt(re * re + im * im), 0.25)
-        linear = linear + re
-        phase_re = phase_re + re * inverse
-        phase_im = phase_im + im * inverse
+        if s == 0:
+            linear, phase_re, phase_im = re, re * inverse, im * inverse
+        else:
+            linear = linear + re
+            phase_re = phase_re + re * inverse
+            phase_im = phase_im + im * inverse
     coherence = jnp.sqrt(phase_re * phase_re + phase_im * phase_im)
     pws = linear * coherence * (1.0 / segments)
-    out_ref[:, :N1] = pws[:PAIRS, :N1]
-    out_ref[:, N1:] = pws[PAIRS : 2 * PAIRS, :N1]
+    for n in range(2):
+        low = pws[n * PAIRS : (n + 1) * PAIRS]
+        high = pws[(2 + n) * PAIRS : (3 + n) * PAIRS]
+        out_ref[:, n * N1 : (n + 1) * N1] = jnp.concatenate([low, high], 1)[:, :N1]
 
 
 def stack_call(x):

time: 98.1 us -> 96.3 us (0.982)
  blocking collectives: 86.8 us -> 85.8 us
    all_to_all x1, blocking collectives: 26.6 us -> 25.6 us  [local(): lags = lax.all_to_all(lags, 'seg', split_axis=0, concat_axis=0, tiled=True)]
where the time goes in v6:
time: 96.3 us; the launch traced here: 95.7 us
  blocking collectives  85.8 us (89%)
  Pallas kernels  9.87 us (10%)
    all_to_all x1, blocking collectives, local(): lax.all_to_all(chosen, ('near', 'cell'), split_axis=0, concat_axis=0, til...  34.5 us
    all_to_all x1, blocking collectives, local(): lax.all_to_all(whitened, 'far', split_axis=0, concat_axis=0, tiled=True)  25.7 us
    all_to_all x1, blocking collectives, local(): lags = lax.all_to_all(lags, 'seg', split_axis=0, concat_axis=0, tiled=True)  25.6 us
    pallas_call x1, Pallas kernels, lag_call(): pl.pallas_call(lag_kernel, out_shape=jax.ShapeDtypeStruct((H, LAGROWS, 12...  4.5 us
    pallas_call x1, Pallas kernels, spectrum_call(): pl.pallas_call(spectrum_kernel, out_shape=jax.ShapeDtypeStruct((FAR, STAT...  3.78 us

profile of v6, /device:TPU:6, one launch (start us, length us, event | category | flops | bytes accessed | tf_op | source)
XLA Modules:
  0.0 95.7 jit_solution(2903872822348034667)
XLA Ops:
  0.0 3.8 %spectrum.1 = bf16[4,4,152,128]{3,2,1,0:T(8,128)(2,1)} custom-call(s32[64]{0:T(128)} %bitcast.5, bf16[1,4,72000]{2,1,0:T(4,128)(2,1)} %x_hbm.1, bf16[608,320]{1,0:T(8,128)(2,1)} %constant.12.clone.dft_hbm, bf16[2,304,240]{2,1,0:T(8,128)(2,1)} %constant.13.clone.twist_hbm, bf16[2,240,128]{2,1,0:T(8,128)(2,1)} %constant.14.clone.last_hbm), custom_call_target="tpu_custom_call" | custom-call | tf_op jit(solution)/shard_map/spectrum/pallas_call | solution.py:158
  3.8 25.7 %all_to_all.15.x_ref = bf16[4,4,152,128]{3,2,1,0:T(8,128)(2,1)S(1)} all-to-all(bf16[4,4,152,128]{3,2,1,0:T(8,128)(2,1)} %spectrum.1), channel_id=1, replica_groups=mesh['far'=4,'near'=2,'cell'=8,'seg'=8] {'far'}, dimensions={0} | all-to-all | bytes 1245184 | tf_op jit(solution)/shard_map/all_to_all | solution.py:314
  29.4 0.6 choose.1
  30.0 0.0 copy-start
  30.1 0.0 copy-start.1
  30.1 0.0 copy-start.2
  30.1 0.0 copy-start.3
  30.1 34.5 %all_to_all.16 = bf16[16,4,152,128]{3,2,1,0:T(8,128)(2,1)S(1)} all-to-all(bf16[16,4,152,128]{3,2,1,0:T(8,128)(2,1)S(1)} %choose.1), channel_id=1, replica_groups=mesh['far'=4,'near'=2,'cell'=8,'seg'=8] {'near','cell'}, dimensions={0} | all-to-all | bytes 4980736 | tf_op jit(solution)/shard_map/all_to_all | solution.py:316
  64.6 0.0 copy-done
  64.6 0.0 copy-done.1
  64.6 0.0 copy-done.2
  64.6 0.0 copy-done.3
  64.6 4.5 %lags.1 = bf16[8,200,128]{2,1,0:T(8,128)(2,1)S(1)} custom-call(s32[26]{0:T(128)S(1)} %bitcast.4, bf16[64,152,128]{2,1,0:T(8,128)(2,1)S(1)} %bitcast.3, bf16[256,1024]{1,0:T(8,128)(2,1)S(1)} %copy-done, bf16[2,2,152,256]{3,2,1,0:T(8,128)(2,1)S(1)} %copy-done.1, bf16[32,304]{1,0:T(8,128)(2,1)S(1)} %copy-done.2), custom_call_target="tpu_custom_call" | custom-call | tf_op jit(solution)/shard_map/lags/pallas_call | solution.py:261
  69.1 25.6 %all_to_all.17.x_ref = bf16[8,200,128]{2,1,0:T(8,128)(2,1)S(1)} all-to-all(bf16[8,200,128]{2,1,0:T(8,128)(2,1)S(1)} %lags.1), channel_id=1, replica_groups=mesh['far'=4,'near'=2,'cell'=8,'seg'=8] {'seg'}, dimensions={0} | all-to-all | bytes 819200 | tf_op jit(solution)/shard_map/all_to_all | solution.py:318
  94.7 1.0 %stack.1 = f32[25,480]{1,0:T(8,128)} custom-call(bf16[8,200,128]{2,1,0:T(8,128)(2,1)S(1)} %all_to_all.17.x_ref), custom_call_target="tpu_custom_call" | custom-call | tf_op jit(solution)/shard_map/stack/pallas_call | solution.py:300
Async XLA Ops:
  30.0 34.5 %copy-start = (bf16[256,1024]{1,0:T(8,128)(2,1)S(1)}, bf16[256,1024]{1,0:T(8,128)(2,1)}, u32[]{:S(2)}) copy-start(bf16[256,1024]{1,0:T(8,128)(2,1)} %constant.15.clone.back_ref) | copy-start | bytes 1572868
  30.1 34.5 %copy-start.1 = (bf16[2,2,152,256]{3,2,1,0:T(8,128)(2,1)S(1)}, bf16[2,2,152,256]{3,2,1,0:T(8,128)(2,1)}, u32[]{:S(2)}) copy-start(bf16[2,2,152,256]{3,2,1,0:T(8,128)(2,1)} %constant.16.clone.twist_ref) | copy-start | bytes 933892
  30.1 34.5 %copy-start.2 = (bf16[32,304]{1,0:T(8,128)(2,1)S(1)}, bf16[32,304]{1,0:T(8,128)(2,1)}, u32[]{:S(2)}) copy-start(bf16[32,304]{1,0:T(8,128)(2,1)} %constant.17.clone.lag_ref) | copy-start | bytes 58372
  30.1 34.5 %copy-start.3 = (s32[1,26]{1,0:T(1,128)S(1)}, s32[1,26]{1,0:T(1,128)}, u32[]{:S(2)}) copy-start(s32[1,26]{1,0:T(1,128)} %param.10) | copy-start | bytes 316

commit v7 on v6

--- a/solution.py
+++ b/solution.py
@@ -157,7 +157,7 @@
     hbm = pl.BlockSpec(memory_space=pl.ANY)
     return pl.pallas_call(
         spectrum_kernel,
-        out_shape=jax.ShapeDtypeStruct((FAR, STATIONS, ROWS, 2 * HALF), jnp.bfloat16),
+        out_shape=pltpu.VMEM((FAR, STATIONS, ROWS, 2 * HALF), jnp.bfloat16),
         in_specs=[hbm, hbm, hbm, hbm, hbm],
         out_specs=vmem,
         scratch_shapes=[
@@ -169,7 +169,7 @@
             pltpu.VMEM(last.shape, jnp.bfloat16),
             pltpu.SemaphoreType.DMA((5,)),
         ],
-        compiler_params=pltpu.CompilerParams(vmem_limit_bytes=60 * 2**20),
+        compiler_params=pltpu.CompilerParams(vmem_limit_bytes=56 * 2**20),
         name="spectrum",
     )(pick, x, jnp.asarray(dft), jnp.asarray(twist), jnp.asarray(last))
 

time: 96.3 us -> 95.4 us (level)
  no operation moved by 1% of the time
where the time goes in v7:
time: 95.4 us; the launch traced here: 94.8 us
  blocking collectives  85.6 us (90%)
  Pallas kernels  9.13 us (10%)
    all_to_all x1, blocking collectives, local(): lax.all_to_all(chosen, ('near', 'cell'), split_axis=0, concat_axis=0, til...  34.5 us
    all_to_all x1, blocking collectives, local(): lags = lax.all_to_all(lags, 'seg', split_axis=0, concat_axis=0, tiled=True)  25.6 us
    all_to_all x1, blocking collectives, local(): lax.all_to_all(whitened, 'far', split_axis=0, concat_axis=0, tiled=True)  25.5 us
    pallas_call x1, Pallas kernels, lag_call(): pl.pallas_call(lag_kernel, out_shape=jax.ShapeDtypeStruct((H, LAGROWS, 12...  4.6 us
    pallas_call x1, Pallas kernels, spectrum_call(): pl.pallas_call(spectrum_kernel, out_shape=pltpu.VMEM((FAR, STATIONS, ROWS...  2.94 us

profile of v7, /device:TPU:6, one launch (start us, length us, event | category | flops | bytes accessed | tf_op | source)
XLA Modules:
  0.0 94.8 jit_solution(12707788828075968787)
XLA Ops:
  0.0 2.9 %spectrum.1 = bf16[4,4,152,128]{3,2,1,0:T(8,128)(2,1)S(1)} custom-call(s32[64]{0:T(128)} %bitcast.5, bf16[1,4,72000]{2,1,0:T(4,128)(2,1)} %x_hbm.1, bf16[608,320]{1,0:T(8,128)(2,1)} %constant.12.clone.dft_hbm, bf16[2,304,240]{2,1,0:T(8,128)(2,1)} %constant.13.clone.twist_hbm, bf16[2,240,128]{2,1,0:T(8,128)(2,1)} %constant.14.clone.last_hbm), custom_call_target="tpu_custom_call" | custom-call | tf_op jit(solution)/shard_map/spectrum/pallas_call | solution.py:158
  2.9 25.5 %all_to_all.15.x_ref = bf16[4,4,152,128]{3,2,1,0:T(8,128)(2,1)S(1)} all-to-all(bf16[4,4,152,128]{3,2,1,0:T(8,128)(2,1)S(1)} %spectrum.1), channel_id=1, replica_groups=mesh['far'=4,'near'=2,'cell'=8,'seg'=8] {'far'}, dimensions={0} | all-to-all | bytes 1245184 | tf_op jit(solution)/shard_map/all_to_all | solution.py:314
  28.4 0.6 choose.1
  29.0 0.0 copy-start
  29.0 0.0 copy-start.1
  29.0 0.0 copy-start.2
  29.0 0.0 copy-start.3
  29.1 34.5 %all_to_all.16 = bf16[16,4,152,128]{3,2,1,0:T(8,128)(2,1)S(1)} all-to-all(bf16[16,4,152,128]{3,2,1,0:T(8,128)(2,1)S(1)} %choose.1), channel_id=1, replica_groups=mesh['far'=4,'near'=2,'cell'=8,'seg'=8] {'near','cell'}, dimensions={0} | all-to-all | bytes 4980736 | tf_op jit(solution)/shard_map/all_to_all | solution.py:316
  63.5 0.0 copy-done
  63.5 0.0 copy-done.1
  63.5 0.0 copy-done.2
  63.5 0.0 copy-done.3
  63.6 4.6 %lags.1 = bf16[8,200,128]{2,1,0:T(8,128)(2,1)S(1)} custom-call(s32[26]{0:T(128)S(1)} %bitcast.4, bf16[64,152,128]{2,1,0:T(8,128)(2,1)S(1)} %bitcast.3, bf16[256,1024]{1,0:T(8,128)(2,1)S(1)} %copy-done, bf16[2,2,152,256]{3,2,1,0:T(8,128)(2,1)S(1)} %copy-done.1, bf16[32,304]{1,0:T(8,128)(2,1)S(1)} %copy-done.2), custom_call_target="tpu_custom_call" | custom-call | tf_op jit(solution)/shard_map/lags/pallas_call | solution.py:261
  68.2 25.6 %all_to_all.17.x_ref = bf16[8,200,128]{2,1,0:T(8,128)(2,1)S(1)} all-to-all(bf16[8,200,128]{2,1,0:T(8,128)(2,1)S(1)} %lags.1), channel_id=1, replica_groups=mesh['far'=4,'near'=2,'cell'=8,'seg'=8] {'seg'}, dimensions={0} | all-to-all | bytes 819200 | tf_op jit(solution)/shard_map/all_to_all | solution.py:318
  93.8 1.0 %stack.1 = f32[25,480]{1,0:T(8,128)} custom-call(bf16[8,200,128]{2,1,0:T(8,128)(2,1)S(1)} %all_to_all.17.x_ref), custom_call_target="tpu_custom_call" | custom-call | tf_op jit(solution)/shard_map/stack/pallas_call | solution.py:300
Async XLA Ops:
  29.0 34.5 %copy-start = (bf16[256,1024]{1,0:T(8,128)(2,1)S(1)}, bf16[256,1024]{1,0:T(8,128)(2,1)}, u32[]{:S(2)}) copy-start(bf16[256,1024]{1,0:T(8,128)(2,1)} %constant.15.clone.back_ref) | copy-start | bytes 1572868
  29.0 34.5 %copy-start.1 = (bf16[2,2,152,256]{3,2,1,0:T(8,128)(2,1)S(1)}, bf16[2,2,152,256]{3,2,1,0:T(8,128)(2,1)}, u32[]{:S(2)}) copy-start(bf16[2,2,152,256]{3,2,1,0:T(8,128)(2,1)} %constant.16.clone.twist_ref) | copy-start | bytes 933892
  29.0 34.5 %copy-start.2 = (bf16[32,304]{1,0:T(8,128)(2,1)S(1)}, bf16[32,304]{1,0:T(8,128)(2,1)}, u32[]{:S(2)}) copy-start(bf16[32,304]{1,0:T(8,128)(2,1)} %constant.17.clone.lag_ref) | copy-start | bytes 58372
  29.0 34.5 %copy-start.3 = (s32[1,26]{1,0:T(1,128)S(1)}, s32[1,26]{1,0:T(1,128)}, u32[]{:S(2)}) copy-start(s32[1,26]{1,0:T(1,128)} %param.10) | copy-start | bytes 316

commit v8 on v7

--- a/solution.py
+++ b/solution.py
@@ -26,7 +26,7 @@
 STEP = FOLD * N1
 FULL = N2 // FOLD
 STAGED = 40
-TAIL = 148
+MID = N2 // 2
 
 
 def angles(left, right, period):
@@ -36,6 +36,11 @@
 
 def bf(table):
     return np.asarray(table, np.float32).astype(jnp.bfloat16)
+
+
+def bins(h):
+    at = np.arange(h, MID + 1 - h)
+    return at, (N2 - at if h else at)
 
 
 def forward_tables():
@@ -43,14 +48,16 @@
     outer = np.arange(N1)
     band = np.arange(1, KB + 1)
     a = angles(inner, inner, N2)
-    dft = np.zeros((4 * ROWS, FOLD * STAGED), np.float32)
+    dft = np.zeros((2 * ROWS, FOLD * STAGED), np.float32)
     column = inner % FOLD * STAGED + inner // FOLD
-    dft[:N2, column] = np.cos(a)
-    dft[2 * ROWS : 2 * ROWS + N2, column] = -np.sin(a)
+    dft[: MID + 1, column] = np.cos(a[: MID + 1])
+    dft[ROWS : ROWS + MID + 1, column] = -np.sin(a[: MID + 1])
     t = angles(inner, outer, N1 * N2)
-    twist = np.zeros((2, 2 * ROWS, N1), np.float32)
-    twist[0, :N2] = np.cos(t)
-    twist[1, :N2] = np.sin(t)
+    twist = np.zeros((2, 2, ROWS, N1), np.float32)
+    for h in range(2):
+        at, k2 = bins(h)
+        twist[h, 0, at] = np.cos(t[k2])
+        twist[h, 1, at] = np.sin(t[k2])
     o = angles(outer, band, N1)
     c, s = np.cos(o), np.sin(o)
     last = np.stack([np.concatenate([c, -s, c, -s], 1), np.concatenate([s, c, s, c], 1)])
@@ -78,15 +85,15 @@
     t = angles(inner, outer, N1 * N2)
     twist = np.zeros((2, 2, ROWS, WIDE), np.float32)
     for h in range(2):
-        n = min(ROWS, N2 - h * ROWS)
-        twist[h, 0, :n, :N1] = np.cos(t[h * ROWS : h * ROWS + n])
-        twist[h, 1, :n, :N1] = np.sin(t[h * ROWS : h * ROWS + n])
+        at, k2 = bins(h)
+        twist[h, 0, at, :N1] = np.cos(t[k2])
+        twist[h, 1, at, :N1] = np.sin(t[k2])
     l = angles(np.arange(-H, H) % N2, inner, N2)
     lag = np.zeros((2, 4 * H, ROWS), np.float32)
     for h in range(2):
-        n = min(ROWS, N2 - h * ROWS)
-        lag[h, : 2 * H, :n] = np.cos(l[:, h * ROWS : h * ROWS + n])
-        lag[h, 2 * H :, :n] = np.sin(l[:, h * ROWS : h * ROWS + n])
+        at, k2 = bins(h)
+        lag[h, : 2 * H, at] = np.cos(l[:, k2]).T
+        lag[h, 2 * H :, at] = np.sin(l[:, k2]).T
     return bf(back), bf(twist), bf(np.concatenate([lag[0], lag[1]], 1))
 
 
@@ -120,8 +127,7 @@
         stage[c, FULL * STATIONS : (FULL + 1) * STATIONS] = rest[:, c * 128 : (c + 1) * 128]
     for copy in copies[1:]:
         copy.wait()
-    cosine = twist_ref[0].astype(jnp.float32)
-    sine = twist_ref[1].astype(jnp.float32)
+    turns = [[twist_ref[h, i].astype(jnp.float32) for i in range(2)] for h in range(2)]
     lane = lax.broadcasted_iota(jnp.int32, (ROWS, 2 * HALF), 1)
     reals, imags = [], []
     for t in range(STATIONS):
@@ -129,13 +135,15 @@
         rows = jnp.concatenate([stage.at[c][at] for c in range(tiles)], 1)
         v = jnp.concatenate([rows[:, r * N1 : (r + 1) * N1] for r in range(FOLD)], 0)
         y = jnp.dot(dft_ref[...], v.astype(jnp.bfloat16), preferred_element_type=jnp.float32)
-        re, im = y[: 2 * ROWS], y[2 * ROWS :]
-        reals.append((re * cosine + im * sine).astype(jnp.bfloat16))
-        imags.append((im * cosine - re * sine).astype(jnp.bfloat16))
+        re, im = y[:ROWS], y[ROWS:]
+        for (cosine, sine), conjugate in zip(turns, (im, -im)):
+            reals.append((re * cosine + conjugate * sine).astype(jnp.bfloat16))
+            imags.append((conjugate * cosine - re * sine).astype(jnp.bfloat16))
     spectra = jnp.dot(jnp.concatenate(reals, 0), last_ref[0], preferred_element_type=jnp.float32)
     spectra = spectra + jnp.dot(jnp.concatenate(imags, 0), last_ref[1], preferred_element_type=jnp.float32)
-    row = lax.broadcasted_iota(jnp.int32, (8, 2 * HALF), 0) + (ROWS - 8)
+    row = lax.broadcasted_iota(jnp.int32, (8, 2 * HALF), 0)
     upper = lax.broadcasted_iota(jnp.int32, (8, 2 * HALF), 1) >= HALF
+    spare = [(row == 0) & upper, (row == 6) & upper, (row == 7) & upper, (row == 7) & ~upper]
     for t in range(STATIONS):
         x = spectra[2 * ROWS * t : 2 * ROWS * (t + 1)]
         power = x * x
@@ -144,11 +152,12 @@
         w = x * (1.0 / level)
         packed = jnp.where(lane < HALF, w[:ROWS], w[ROWS:])
         for f in range(FAR):
-            tail = packed[ROWS - 8 :]
+            ends = [packed[:8], packed[ROWS - 8 :]]
             for i in range(NEAR // STATIONS):
                 wanted = pick_ref[f * NEAR + t * (NEAR // STATIONS) + i].astype(jnp.float32)
-                tail = jnp.where((row == TAIL + i) & upper, wanted, tail)
-            out_ref[f, t] = jnp.concatenate([packed[: ROWS - 8], tail], 0).astype(jnp.bfloat16)
+                ends[i > 0] = jnp.where(spare[i], wanted, ends[i > 0])
+            whole = jnp.concatenate([ends[0], packed[8 : ROWS - 8], ends[1]], 0)
+            out_ref[f, t] = whole.astype(jnp.bfloat16)
 
 
 def spectrum_call(pick, x):
@@ -178,11 +187,15 @@
     lane = lax.broadcasted_iota(jnp.int32, (8, 2 * HALF), 1)
     for f in range(FAR):
         wanted = []
-        for d in range(NEAR):
-            tail = x_ref[f, d // 4, ROWS - 8 :].astype(jnp.float32)
-            tail = jnp.where(lane < HALF, pltpu.roll(tail, HALF, 1), tail)
-            row = TAIL - ROWS + 8 + d % 4
-            wanted.append(jnp.broadcast_to(tail[row : row + 1], (16, 2 * HALF)).astype(jnp.bfloat16))
+        for t in range(STATIONS):
+            head = x_ref[f, t, :16].astype(jnp.float32)[:8]
+            tail = x_ref[f, t, ROWS - 8 :].astype(jnp.float32)
+            head = jnp.where(lane < HALF, pltpu.roll(head, HALF, 1), head)
+            turned = pltpu.roll(tail, HALF, 1)
+            upper = jnp.where(lane < HALF, turned, tail)
+            lower = jnp.where(lane < HALF, tail, turned)
+            for line in (head[:1], upper[6:7], upper[7:], lower[7:]):
+                wanted.append(jnp.broadcast_to(line, (16, 2 * HALF)).astype(jnp.bfloat16))
         for k in range(0, ROWS, 16):
             n = min(16, ROWS - k)
             parts = [x_ref[f, t, k : k + n] for t in range(STATIONS)]
@@ -280,7 +293,7 @@
     for s in range(segments):
         x = x_ref[s].astype(jnp.float32)
         re, im = x[:half], x[half:]
-        inverse = 1.0 / jnp.maximum(jnp.sqrt(re * re + im * im), 0.25)
+        inverse = jnp.minimum(lax.rsqrt(re * re + im * im), 4.0)
         if s == 0:
             linear, phase_re, phase_im = re, re * inverse, im * inverse
         else:

time: 95.4 us -> 95 us (level)
  no operation moved by 1% of the time
where the time goes in v8:
time: 95 us; the launch traced here: 94.4 us
  blocking collectives  85.6 us (90%)
  Pallas kernels  8.78 us (9%)
    all_to_all x1, blocking collectives, local(): lax.all_to_all(chosen, ('near', 'cell'), split_axis=0, concat_axis=0, til...  34.5 us
    all_to_all x1, blocking collectives, local(): lags = lax.all_to_all(lags, 'seg', split_axis=0, concat_axis=0, tiled=True)  25.6 us
    all_to_all x1, blocking collectives, local(): lax.all_to_all(whitened, 'far', split_axis=0, concat_axis=0, tiled=True)  25.5 us
    pallas_call x1, Pallas kernels, lag_call(): pl.pallas_call(lag_kernel, out_shape=jax.ShapeDtypeStruct((H, LAGROWS, 12...  4.6 us
    pallas_call x1, Pallas kernels, spectrum_call(): pl.pallas_call(spectrum_kernel, out_shape=pltpu.VMEM((FAR, STATIONS, ROWS...  2.66 us

profile of v8, /device:TPU:6, one launch (start us, length us, event | category | flops | bytes accessed | tf_op | source)
XLA Modules:
  0.0 94.4 jit_solution(1001896726573828290)
XLA Ops:
  0.0 2.7 %spectrum.1 = bf16[4,4,152,128]{3,2,1,0:T(8,128)(2,1)S(1)} custom-call(s32[64]{0:T(128)} %bitcast.5, bf16[1,4,72000]{2,1,0:T(4,128)(2,1)} %x_hbm.1, bf16[304,320]{1,0:T(8,128)(2,1)} %constant.12.clone.dft_hbm, bf16[2,2,152,240]{3,2,1,0:T(8,128)(2,1)} %constant.13.clone.twist_hbm, bf16[2,240,128]{2,1,0:T(8,128)(2,1)} %constant.14.clone.last_hbm), custom_call_target="tpu_custom_call" | custom-call | tf_op jit(solution)/shard_map/spectrum/pallas_call | solution.py:167
  2.7 25.5 %all_to_all.15.x_ref = bf16[4,4,152,128]{3,2,1,0:T(8,128)(2,1)S(1)} all-to-all(bf16[4,4,152,128]{3,2,1,0:T(8,128)(2,1)S(1)} %spectrum.1), channel_id=1, replica_groups=mesh['far'=4,'near'=2,'cell'=8,'seg'=8] {'far'}, dimensions={0} | all-to-all | bytes 1245184 | tf_op jit(solution)/shard_map/all_to_all | solution.py:327
  28.1 0.6 choose.1
  28.7 0.0 copy-start
  28.7 0.0 copy-start.1
  28.8 0.0 copy-start.2
  28.8 0.0 copy-start.3
  28.8 34.5 %all_to_all.16 = bf16[16,4,152,128]{3,2,1,0:T(8,128)(2,1)S(1)} all-to-all(bf16[16,4,152,128]{3,2,1,0:T(8,128)(2,1)S(1)} %choose.1), channel_id=1, replica_groups=mesh['far'=4,'near'=2,'cell'=8,'seg'=8] {'near','cell'}, dimensions={0} | all-to-all | bytes 4980736 | tf_op jit(solution)/shard_map/all_to_all | solution.py:329
  63.3 0.0 copy-done
  63.3 0.0 copy-done.1
  63.3 0.0 copy-done.2
  63.3 0.0 copy-done.3
  63.3 4.6 %lags.1 = bf16[8,200,128]{2,1,0:T(8,128)(2,1)S(1)} custom-call(s32[26]{0:T(128)S(1)} %bitcast.4, bf16[64,152,128]{2,1,0:T(8,128)(2,1)S(1)} %bitcast.3, bf16[256,1024]{1,0:T(8,128)(2,1)S(1)} %copy-done, bf16[2,2,152,256]{3,2,1,0:T(8,128)(2,1)S(1)} %copy-done.1, bf16[32,304]{1,0:T(8,128)(2,1)S(1)} %copy-done.2), custom_call_target="tpu_custom_call" | custom-call | tf_op jit(solution)/shard_map/lags/pallas_call | solution.py:274
  67.9 25.6 %all_to_all.17.x_ref = bf16[8,200,128]{2,1,0:T(8,128)(2,1)S(1)} all-to-all(bf16[8,200,128]{2,1,0:T(8,128)(2,1)S(1)} %lags.1), channel_id=1, replica_groups=mesh['far'=4,'near'=2,'cell'=8,'seg'=8] {'seg'}, dimensions={0} | all-to-all | bytes 819200 | tf_op jit(solution)/shard_map/all_to_all | solution.py:331
  93.5 0.9 stack.1
Async XLA Ops:
  28.7 34.5 %copy-start = (bf16[256,1024]{1,0:T(8,128)(2,1)S(1)}, bf16[256,1024]{1,0:T(8,128)(2,1)}, u32[]{:S(2)}) copy-start(bf16[256,1024]{1,0:T(8,128)(2,1)} %constant.15.clone.back_ref) | copy-start | bytes 1572868
  28.7 34.5 %copy-start.1 = (bf16[2,2,152,256]{3,2,1,0:T(8,128)(2,1)S(1)}, bf16[2,2,152,256]{3,2,1,0:T(8,128)(2,1)}, u32[]{:S(2)}) copy-start(bf16[2,2,152,256]{3,2,1,0:T(8,128)(2,1)} %constant.16.clone.twist_ref) | copy-start | bytes 933892
  28.8 34.5 %copy-start.2 = (bf16[32,304]{1,0:T(8,128)(2,1)S(1)}, bf16[32,304]{1,0:T(8,128)(2,1)}, u32[]{:S(2)}) copy-start(bf16[32,304]{1,0:T(8,128)(2,1)} %constant.17.clone.lag_ref) | copy-start | bytes 58372
  28.8 34.5 %copy-start.3 = (s32[1,26]{1,0:T(1,128)S(1)}, s32[1,26]{1,0:T(1,128)}, u32[]{:S(2)}) copy-start(s32[1,26]{1,0:T(1,128)} %param.10) | copy-start | bytes 316

commit v9 on v8

--- a/solution.py
+++ b/solution.py
@@ -89,12 +89,12 @@
         twist[h, 0, at, :N1] = np.cos(t[k2])
         twist[h, 1, at, :N1] = np.sin(t[k2])
     l = angles(np.arange(-H, H) % N2, inner, N2)
-    lag = np.zeros((2, 4 * H, ROWS), np.float32)
-    for h in range(2):
-        at, k2 = bins(h)
-        lag[h, : 2 * H, at] = np.cos(l[:, k2]).T
-        lag[h, 2 * H :, at] = np.sin(l[:, k2]).T
-    return bf(back), bf(twist), bf(np.concatenate([lag[0], lag[1]], 1))
+    lag = np.zeros((2, 2 * H, 2, ROWS), np.float32)
+    at = np.arange(MID + 1)
+    c, s = np.cos(l[:, at]), np.sin(l[:, at])
+    lag[0, :, 0, at], lag[0, :, 1, at] = c.T, -s.T
+    lag[1, :, 0, at], lag[1, :, 1, at] = c.T, s.T
+    return bf(back), bf(twist), bf(lag.reshape(2, 2 * H, 2 * ROWS))
 
 
 def spectrum_kernel(
@@ -222,7 +222,7 @@
     return (owner & (NEAR - 1)) * FAR + (owner >> 4)
 
 
-def lag_kernel(row_ref, w_ref, back_ref, twist_ref, lag_ref, out_ref, stage, gather, product):
+def lag_kernel(row_ref, w_ref, back_ref, twist_ref, lag_ref, out_ref, stage, product):
     lane = lax.broadcasted_iota(jnp.int32, (ROWS, 2 * HALF), 1) % HALF
     s = w_ref[place(row_ref[0])].astype(jnp.float32)
     s1 = jnp.where(lane < KB, s, pltpu.roll(s, KB, 1)).astype(jnp.bfloat16)
@@ -246,26 +246,26 @@
             re, im = mine[:, :WIDE], mine[:, WIDE:]
             a = re * cosine - im * sine
             b = re * sine + im * cosine
-            turned[i].append(jnp.concatenate([a, b], 1))
+            turned[i].append((a, b))
     for i in range(PAIRS):
-        total = jnp.dot(
-            lag_ref[...],
-            jnp.concatenate(turned[i], 0),
-            preferred_element_type=jnp.float32,
+        (a0, b0), (a1, b1) = turned[i]
+        sides = (a0 + a1, b0 - b1), (b0 + b1, a0 - a1)
+        re, im = (
+            jnp.dot(lag_ref[k], jnp.concatenate(side, 0), preferred_element_type=jnp.float32) * scale
+            for k, side in enumerate(sides)
         )
-        re = (total[: 2 * H, :WIDE] - total[2 * H :, WIDE:]) * scale
-        im = (total[2 * H :, :WIDE] + total[: 2 * H, WIDE:]) * scale
         at = pl.ds(i * 2 * H, 2 * H)
         for lanes in range(2):
             stage[lanes, at] = re[:, lanes * 128 : (lanes + 1) * 128]
             stage[2 + lanes, at] = im[:, lanes * 128 : (lanes + 1) * 128]
 
     for j in range(H):
-        for lanes in range(4):
-            for n in range(2):
-                rows = stage.at[lanes][pl.ds(2 * j + n, PAIRS, stride=2 * H)]
-                gather[pl.ds((2 * lanes + n) * PAIRS, PAIRS)] = rows
-        out_ref[j] = gather[...].astype(jnp.bfloat16)
+        rows = [
+            stage.at[lanes][pl.ds(2 * j + n, PAIRS, stride=2 * H)]
+            for lanes in range(4)
+            for n in range(2)
+        ]
+        out_ref[j] = jnp.concatenate(rows, 0).astype(jnp.bfloat16)
 
 
 def lag_call(rows, w):
@@ -278,7 +278,6 @@
         out_specs=vmem,
         scratch_shapes=[
             pltpu.VMEM((4, PAIRS * 2 * H, 128), jnp.float32),
-            pltpu.VMEM((LAGROWS, 128), jnp.float32),
             pltpu.VMEM((PAIRS, PITCH, 4 * HALF), jnp.bfloat16),
         ],
         compiler_params=pltpu.CompilerParams(vmem_limit_bytes=48 * 2**20),

time: 95 us -> 95 us (level)
  no operation moved by 1% of the time
where the time goes in v9:
time: 95 us; the launch traced here: 94.4 us
  blocking collectives  85.6 us (90%)
  Pallas kernels  8.73 us (9%)
    all_to_all x1, blocking collectives, local(): lax.all_to_all(chosen, ('near', 'cell'), split_axis=0, concat_axis=0, til...  34.5 us
    all_to_all x1, blocking collectives, local(): lags = lax.all_to_all(lags, 'seg', split_axis=0, concat_axis=0, tiled=True)  25.6 us
    all_to_all x1, blocking collectives, local(): lax.all_to_all(whitened, 'far', split_axis=0, concat_axis=0, tiled=True)  25.5 us
    pallas_call x1, Pallas kernels, lag_call(): pl.pallas_call(lag_kernel, out_shape=jax.ShapeDtypeStruct((H, LAGROWS, 12...  4.55 us
    pallas_call x1, Pallas kernels, spectrum_call(): pl.pallas_call(spectrum_kernel, out_shape=pltpu.VMEM((FAR, STATIONS, ROWS...  2.66 us

profile of v9, /device:TPU:6, one launch (start us, length us, event | category | flops | bytes accessed | tf_op | source)
XLA Modules:
  0.0 94.4 jit_solution(4427178230001414376)
XLA Ops:
  0.0 2.7 %spectrum.1 = bf16[4,4,152,128]{3,2,1,0:T(8,128)(2,1)S(1)} custom-call(s32[64]{0:T(128)} %bitcast.5, bf16[1,4,72000]{2,1,0:T(4,128)(2,1)} %x_hbm.1, bf16[304,320]{1,0:T(8,128)(2,1)} %constant.12.clone.dft_hbm, bf16[2,2,152,240]{3,2,1,0:T(8,128)(2,1)} %constant.13.clone.twist_hbm, bf16[2,240,128]{2,1,0:T(8,128)(2,1)} %constant.14.clone.last_hbm), custom_call_target="tpu_custom_call" | custom-call | tf_op jit(solution)/shard_map/spectrum/pallas_call | solution.py:167
  2.7 25.5 %all_to_all.15.x_ref = bf16[4,4,152,128]{3,2,1,0:T(8,128)(2,1)S(1)} all-to-all(bf16[4,4,152,128]{3,2,1,0:T(8,128)(2,1)S(1)} %spectrum.1), channel_id=1, replica_groups=mesh['far'=4,'near'=2,'cell'=8,'seg'=8] {'far'}, dimensions={0} | all-to-all | bytes 1245184 | tf_op jit(solution)/shard_map/all_to_all | solution.py:326
  28.1 0.6 choose.1
  28.7 0.0 copy-start
  28.7 0.0 copy-start.1
  28.8 0.0 copy-start.2
  28.8 0.0 copy-start.3
  28.8 34.5 %all_to_all.16 = bf16[16,4,152,128]{3,2,1,0:T(8,128)(2,1)S(1)} all-to-all(bf16[16,4,152,128]{3,2,1,0:T(8,128)(2,1)S(1)} %choose.1), channel_id=1, replica_groups=mesh['far'=4,'near'=2,'cell'=8,'seg'=8] {'near','cell'}, dimensions={0} | all-to-all | bytes 4980736 | tf_op jit(solution)/shard_map/all_to_all | solution.py:328
  63.3 0.0 copy-done
  63.3 0.0 copy-done.1
  63.3 0.0 copy-done.2
  63.3 0.0 copy-done.3
  63.3 4.6 %lags.1 = bf16[8,200,128]{2,1,0:T(8,128)(2,1)S(1)} custom-call(s32[26]{0:T(128)S(1)} %bitcast.4, bf16[64,152,128]{2,1,0:T(8,128)(2,1)S(1)} %bitcast.3, bf16[256,1024]{1,0:T(8,128)(2,1)S(1)} %copy-done, bf16[2,2,152,256]{3,2,1,0:T(8,128)(2,1)S(1)} %copy-done.1, bf16[2,16,304]{2,1,0:T(8,128)(2,1)S(1)} %copy-done.2), custom_call_target="tpu_custom_call" | custom-call | tf_op jit(solution)/shard_map/lags/pallas_call | solution.py:274
  67.9 25.6 %all_to_all.17.x_ref = bf16[8,200,128]{2,1,0:T(8,128)(2,1)S(1)} all-to-all(bf16[8,200,128]{2,1,0:T(8,128)(2,1)S(1)} %lags.1), channel_id=1, replica_groups=mesh['far'=4,'near'=2,'cell'=8,'seg'=8] {'seg'}, dimensions={0} | all-to-all | bytes 819200 | tf_op jit(solution)/shard_map/all_to_all | solution.py:330
  93.5 0.9 stack.1
Async XLA Ops:
  28.7 34.5 %copy-start = (bf16[256,1024]{1,0:T(8,128)(2,1)S(1)}, bf16[256,1024]{1,0:T(8,128)(2,1)}, u32[]{:S(2)}) copy-start(bf16[256,1024]{1,0:T(8,128)(2,1)} %constant.15.clone.back_ref) | copy-start | bytes 1572868
  28.7 34.5 %copy-start.1 = (bf16[2,2,152,256]{3,2,1,0:T(8,128)(2,1)S(1)}, bf16[2,2,152,256]{3,2,1,0:T(8,128)(2,1)}, u32[]{:S(2)}) copy-start(bf16[2,2,152,256]{3,2,1,0:T(8,128)(2,1)} %constant.16.clone.twist_ref) | copy-start | bytes 933892
  28.8 34.5 %copy-start.2 = (bf16[2,16,304]{2,1,0:T(8,128)(2,1)S(1)}, bf16[2,16,304]{2,1,0:T(8,128)(2,1)}, u32[]{:S(2)}) copy-start(bf16[2,16,304]{2,1,0:T(8,128)(2,1)} %constant.17.clone.lag_ref) | copy-start | bytes 58372
  28.8 34.5 %copy-start.3 = (s32[1,26]{1,0:T(1,128)S(1)}, s32[1,26]{1,0:T(1,128)}, u32[]{:S(2)}) copy-start(s32[1,26]{1,0:T(1,128)} %param.10) | copy-start | bytes 316
